TPU v7x, 32 devices: a whole 2x2x4 slice. The times are simulated.
32 devices in a mesh: groups: 2 (over y), expert: 4 (over z), dp: 4 (over x, core).
Axes of the slice: x: 2, y: 2, z: 4, core: 2. Of those that a mesh axis runs over, the one named last changes fastest.
Arguments:
- tokens: bfloat16 [4096, 1024], P(('groups', 'expert', 'dp')), parts along dimension 0, may hold values from -6 to 6
- expert_ids: int32 [4096, 8], P(('groups', 'expert', 'dp')), parts along dimension 0, may hold values from 0 to 63, all different within a row; in each aligned block of 128 rows (0 to 127, 128 to 255, ...) at most 16 rows name the same one
- gate_values: float32 [4096, 8], P(('groups', 'expert', 'dp')), parts along dimension 0, may hold values from 0.1 to 1
- w_gate_up: bfloat16 [64, 1024, 768], P('expert', 'dp'), may hold values from -0.1875 to 0.1875
- w_down: bfloat16 [64, 384, 1024], P('expert', None, 'dp'), may hold values from -0.3125 to 0.3125
- new_slot: int32 [64], replicated, may hold values from 0 to 63, each once
- cotangent: bfloat16 [4096, 1024], P(('groups', 'expert', 'dp')), parts along dimension 0, may hold values from -6 to 6
Outputs:
- layer_out: bfloat16 [4096, 1024], P(('groups', 'expert', 'dp')), parts along dimension 0
- d_tokens: bfloat16 [4096, 1024], P(('groups', 'expert', 'dp')), parts along dimension 0
- d_gate_up: bfloat16 [128, 1024, 768], P(('groups', 'expert'), 'dp'), parts along dimension 0
- d_down: bfloat16 [128, 384, 1024], P(('groups', 'expert'), None, 'dp'), parts along dimension 0
There are 2 independent parts, one for each index of `groups`. A program takes and returns all parts, laid end to end along the dimension named above; an argument that names none is the same for every part. Nothing has to cross between parts.
Inputs may be any that keep to these rules, and one draw needn't show every extreme that they name: `expert_ids`: each row names 8 different experts; among the 128 rows of one device no expert is named by more than 16 rows, and on some devices some expert is named by exactly 16. `new_slot`: every number appears once, so each slot holds one expert; slot s belongs to index s // (64 / 4) of axis expert.
All inputs are finite; a program needn't handle non-finite values.
Results may differ from a plain program's by a relative error of at most 0.0095.
Values may be sent and summed in bfloat16 or wider, within the bound.
A program may use at most 192 MiB of HBM per device.

v0:
```python
import jax
import jax.numpy as jnp
from jax import lax
from jax.sharding import PartitionSpec as P

MOST = 16


def relocate(gate_up, down, inverse):
    expert_peers = lax.axis_size("expert")
    home_slots = gate_up.shape[0]
    spread_gu = gate_up.reshape(
        home_slots, expert_peers, gate_up.shape[1] // expert_peers, gate_up.shape[2]
    )
    spread_dn = down.reshape(home_slots, expert_peers, down.shape[1] // expert_peers, down.shape[2])
    got_gu, got_dn = (
        lax.all_to_all(spread_gu, "expert", split_axis=1, concat_axis=0, tiled=True),
        lax.all_to_all(spread_dn, "expert", split_axis=1, concat_axis=0, tiled=True),
    )
    experts = home_slots * expert_peers
    slot_order = inverse.reshape(expert_peers, home_slots).T
    pick_gu = got_gu.reshape(experts, got_gu.shape[2], got_gu.shape[3])[slot_order]
    pick_dn = got_dn.reshape(experts, got_dn.shape[2], got_dn.shape[3])[slot_order]
    new_gu, new_dn = (
        lax.all_to_all(pick_gu, "expert", split_axis=1, concat_axis=1, tiled=True),
        lax.all_to_all(pick_dn, "expert", split_axis=1, concat_axis=1, tiled=True),
    )
    return (new_gu.reshape(gate_up.shape), new_dn.reshape(down.shape))


def route_cells(expert_ids, slot_map):
    experts = slot_map.shape[0]
    flat_ids = expert_ids.reshape(-1)
    matches = flat_ids[:, None] == jnp.arange(experts, dtype=jnp.int32)[None, :]
    indicator = matches.astype(jnp.int32)
    earlier = jnp.cumsum(indicator, axis=0) - indicator
    position = jnp.sum(jnp.where(matches, earlier, 0), axis=1)
    target = jnp.sum(jnp.where(matches, slot_map[None, :], 0), axis=1)
    target_cell = target * MOST + position
    entries = flat_ids.shape[0]
    source = (
        jnp.full((experts * MOST,), entries, jnp.int32)
        .at[target_cell]
        .set(jnp.arange(entries, dtype=jnp.int32))
    )
    return (target_cell, source)


def shards(tokens, expert_ids, gate_values, w_gate_up, w_down, new_slot, cotangent):
    expert_peers = lax.axis_size("expert")
    home_slots = w_gate_up.shape[0]
    model_width = tokens.shape[1]
    hidden_width = w_down.shape[1]
    top_count = expert_ids.shape[1]
    token_count = tokens.shape[0]
    inverse = jnp.argsort(new_slot)
    local_gu, local_dn = relocate(w_gate_up, w_down, inverse)
    full_gu, full_dn = (
        lax.all_gather(local_gu, "dp", axis=1, tiled=True),
        lax.all_gather(local_dn, "dp", axis=2, tiled=True),
    )
    target_cell, source = route_cells(expert_ids, new_slot)
    blank_row = jnp.zeros((1, model_width), jnp.bfloat16)
    token_row = source // top_count
    cell_gates = jnp.concatenate([gate_values.reshape(-1), jnp.zeros((1,), jnp.float32)])[source]
    outgoing = jnp.concatenate([tokens, blank_row], axis=0)[token_row]
    cot_rows = jnp.concatenate([cotangent, blank_row], axis=0)[token_row]
    scaled_cot = (cell_gates[:, None] * cot_rows.astype(jnp.float32)).astype(jnp.bfloat16)
    row_shape = (expert_peers, home_slots, MOST, model_width)
    arrived = lax.all_to_all(
        outgoing.reshape(row_shape), "expert", split_axis=0, concat_axis=0, tiled=True
    )
    gate_up = jnp.einsum("shmd,hdf->shmf", arrived, full_gu, preferred_element_type=jnp.float32)
    gate_part = gate_up[..., :hidden_width]
    up_part = gate_up[..., hidden_width:]
    sigmoid_g = jax.nn.sigmoid(gate_part)
    silu_g = gate_part * sigmoid_g
    activation = (silu_g * up_part).astype(jnp.bfloat16)
    expert_out = jnp.einsum(
        "shmf,hfd->shmd", activation, full_dn, preferred_element_type=jnp.float32
    ).astype(jnp.bfloat16)
    returned = lax.all_to_all(expert_out, "expert", split_axis=0, concat_axis=0, tiled=True)
    gathered_out = returned.reshape(-1, model_width)[target_cell].reshape(
        token_count, top_count, model_width
    )
    layer_out = jnp.sum(gate_values[:, :, None] * gathered_out.astype(jnp.float32), axis=1).astype(
        jnp.bfloat16
    )
    d_outputs = lax.all_to_all(
        scaled_cot.reshape(row_shape), "expert", split_axis=0, concat_axis=0, tiled=True
    )
    d_act = jnp.einsum("shmd,hfd->shmf", d_outputs, full_dn, preferred_element_type=jnp.float32)
    d_gate = d_act * up_part * sigmoid_g * (1.0 + gate_part * (1.0 - sigmoid_g))
    d_up = d_act * silu_g
    d_gate_up = jnp.concatenate([d_gate, d_up], axis=-1).astype(jnp.bfloat16)
    d_rows = jnp.einsum(
        "shmf,hdf->shmd", d_gate_up, full_gu, preferred_element_type=jnp.float32
    ).astype(jnp.bfloat16)
    rows_back = lax.all_to_all(d_rows, "expert", split_axis=0, concat_axis=0, tiled=True)
    gathered_grads = rows_back.reshape(-1, model_width)[target_cell].reshape(
        token_count, top_count, model_width
    )
    d_tokens = jnp.sum(gathered_grads.astype(jnp.float32), axis=1).astype(jnp.bfloat16)
    part_gu = jnp.einsum("shmd,shmf->hdf", arrived, d_gate_up, preferred_element_type=jnp.float32)
    part_dn = jnp.einsum(
        "shmd,shmf->hdf", d_outputs, activation, preferred_element_type=jnp.float32
    )
    sum_gu, sum_dn = (
        lax.psum_scatter(
            part_gu.astype(jnp.bfloat16), "dp", scatter_dimension=1, tiled=True
        ).astype(jnp.float32),
        lax.psum_scatter(
            part_dn.astype(jnp.bfloat16), "dp", scatter_dimension=1, tiled=True
        ).astype(jnp.float32),
    )
    grad_gu = sum_gu.astype(jnp.bfloat16)
    grad_dn = jnp.swapaxes(sum_dn, 1, 2).astype(jnp.bfloat16)
    return (layer_out, d_tokens, grad_gu, grad_dn)


def solution(mesh):
    return jax.shard_map(
        shards,
        mesh=mesh,
        in_specs=(
            P(("groups", "expert", "dp"), None),
            P(("groups", "expert", "dp"), None),
            P(("groups", "expert", "dp"), None),
            P("expert", "dp", None),
            P("expert", None, "dp"),
            P(),
            P(("groups", "expert", "dp"), None),
        ),
        out_specs=(
            P(("groups", "expert", "dp"), None),
            P(("groups", "expert", "dp"), None),
            P(("groups", "expert"), "dp", None),
            P(("groups", "expert"), None, "dp"),
        ),
        check_vma=False,
    )
```

profile of v0, /device:TPU:0, one launch (start us, length us, event | category | flops | bytes accessed | tf_op | source)
XLA Modules:
  0.0 904.9 jit_solution(17954790021503623060)
XLA Ops:
  7.2 6.2 copy.47
  13.4 6.4 all-to-all-start.2
  22.2 136.4 %all-to-all-done.2 = bf16[16,4,64,768]{3,2,0,1:T(8,128)(2,1)} async-done(((bf16[16,4,64,768]{3,2,0,1:T(8,128)(2,1)}), bf16[16,4,64,768]{3,2,0,1:T(8,128)(2,1)}, u32[]{:S(2)}, u32[]{:S(2)}) %all-to-all-start.2) | async-done | bytes 6291488 | tf_op jit(solution)/shard_map/all_to_all | solution.py:17
  158.6 6.4 gather_fusion.1
  165.0 3.2 copy.48
  168.2 140.5 %all_to_all.60 = bf16[16,4,64,768]{3,2,0,1:T(8,128)(2,1)S(1)} all-to-all(bf16[16,4,64,768]{3,2,0,1:T(8,128)(2,1)S(1)} %copy.48), channel_id=1, replica_groups=mesh['groups'=2,'expert'=4,'dp'=4] {'expert'}, dimensions={1} | all-to-all | bytes 12582912 | tf_op jit(solution)/shard_map/all_to_all | solution.py:25
  313.9 72.7 %all_to_all.61 = bf16[16,4,96,256]{3,2,0,1:T(8,128)(2,1)S(1)} all-to-all(bf16[16,4,96,256]{3,2,0,1:T(8,128)(2,1)S(1)} %copy.43), channel_id=1, replica_groups=mesh['groups'=2,'expert'=4,'dp'=4] {'expert'}, dimensions={1} | all-to-all | bytes 6291456 | tf_op jit(solution)/shard_map/all_to_all | solution.py:18
  391.2 72.7 %all_to_all.62 = bf16[16,4,96,256]{3,2,0,1:T(8,128)(2,1)S(1)} all-to-all(bf16[16,4,96,256]{3,2,0,1:T(8,128)(2,1)S(1)} %copy.45), channel_id=1, replica_groups=mesh['groups'=2,'expert'=4,'dp'=4] {'expert'}, dimensions={1} | all-to-all | bytes 6291456 | tf_op jit(solution)/shard_map/all_to_all | solution.py:26
  467.0 18.0 %reduce-window.6 = s32[64,8,128]{2,1,0:T(8,128)S(1)} reduce-window(s32[64,8,128]{2,1,0:T(8,128)S(1)} %fusion.31, s32[]{:T(128)} %constant.11.clone.1), window={size=1x1x128 pad=0_0x0_0x127_0}, to_apply=%region_2.3 | reduce-window | flops 8323072 | bytes 524292 | tf_op jit(solution)/shard_map/reduce-window
  485.8 4.3 scatter_custom_fusion
  490.1 5.3 gather_fusion.2
  495.4 4.6 all-to-all-start.4
  500.3 6.2 gather_fusion.4
  506.5 4.1 gather_fusion.5
  512.4 35.0 %all-to-all-done.4 = bf16[4,16,16,1024]{3,2,1,0:T(8,128)(2,1)} async-done(((bf16[4,16,16,1024]{3,2,1,0:T(8,128)(2,1)}), bf16[4,16,16,1024]{3,2,1,0:T(8,128)(2,1)}, u32[]{:S(2)}, u32[]{:S(2)}) %all-to-all-start.4) | async-done | bytes 2097184 | tf_op jit(solution)/shard_map/all_to_all | solution.py:70
  547.3 3.7 all-to-all-start.6
  551.3 12.6 %fusion.12 = f32[4,16,16,768]{3,2,0,1:T(8,128)} fusion(bf16[4,16,16,1024]{3,2,1,0:T(8,128)(2,1)} %all-to-all-done.4, bf16[16,1024,768]{2,1,0:T(8,128)(2,1)} %all-gather.5.cloned.1.call-done), kind=kOutput, calls=%fused_computation.27 | convolution fusion | flops 1610612736 | bytes 30408704 | tf_op jit(solution)/shard_map/shmd,hdf->shmf/dot_general | solution.py:73
  563.9 34.7 %all-to-all-done.6 = bf16[4,16,16,1024]{3,2,1,0:T(8,128)(2,1)S(1)} async-done(((bf16[4,16,16,1024]{3,2,1,0:T(8,128)(2,1)}), bf16[4,16,16,1024]{3,2,1,0:T(8,128)(2,1)S(1)}, u32[]{:S(2)}, u32[]{:S(2)}) %all-to-all-start.6) | async-done | bytes 2097184 | tf_op jit(solution)/shard_map/all_to_all | solution.py:89
  598.7 10.6 %fusion.23 = (bf16[4,16,16,384]{3,2,0,1:T(8,128)(2,1)S(1)}, bf16[4,16,16,384]{3,2,0,1:T(8,128)(2,1)}, bf16[4,16,16,384]{3,2,0,1:T(8,128)(2,1)}) fusion(f32[4,16,16,768]{3,2,0,1:T(8,128)} %fusion.12, bf16[4,16,16,1024]{3,2,1,0:T(8,128)(2,1)S(1)} %all-to-all-done.6, bf16[16,384,1024]{2,1,0:T(8,128)(2,1)} %all-gather.3.cloned.1.call-done), kind=kOutput, calls=%fused_computation.33 | convolution fusion | flops 811204608 | bytes 20185088 | tf_op jit(solution)/shard_map/shmd,hfd->shmf/dot_general | solution.py:92
  609.3 7.5 bitcast_convert_fusion.1
  617.8 17.1 %bitcast_convert_fusion = bf16[16,1024,768]{2,1,0:T(8,128)(2,1)} fusion(bf16[4,16,16,1024]{3,2,1,0:T(8,128)(2,1)} %all-to-all-done.4, bf16[4,16,16,384]{3,2,0,1:T(8,128)(2,1)S(1)} %copy-done.7, bf16[4,16,16,384]{3,2,0,1:T(8,128)(2,1)S(1)} %get-tuple-element.24), kind=kOutput, calls=%fused_computation.8 | convolution fusion | flops 1626341376 | bytes 28835840 | tf_op jit(solution)/shard_map/shmd,shmf->hdf/dot_general | solution.py:104
  635.0 7.2 convert_bitcast_fusion.1
  643.7 3.8 all-to-all-start.5
  647.6 13.6 %convert_bitcast_fusion = bf16[4,16,16,1024]{3,2,0,1:T(8,128)(2,1)} fusion(bf16[16,1024,768]{2,1,0:T(8,128)(2,1)} %all-gather.5.cloned.1.call-done, bf16[4,16,16,384]{3,2,0,1:T(8,128)(2,1)} %get-tuple-element.25, bf16[4,16,16,384]{3,2,0,1:T(8,128)(2,1)S(1)} %get-tuple-element.24), kind=kOutput, calls=%fused_computation.25 | convolution fusion | flops 1614807040 | bytes 28835840 | tf_op jit(solution)/shard_map/shmf,hdf->shmd/dot_general | solution.py:96
  661.1 3.2 copy.58
  664.4 31.3 %all-to-all-done.5 = bf16[4,16,16,1024]{3,2,1,0:T(8,128)(2,1)S(1)} async-done(((bf16[4,16,16,1024]{3,2,1,0:T(8,128)(2,1)}), bf16[4,16,16,1024]{3,2,1,0:T(8,128)(2,1)S(1)}, u32[]{:S(2)}, u32[]{:S(2)}) %all-to-all-start.5) | async-done | bytes 2097184 | tf_op jit(solution)/shard_map/all_to_all | solution.py:82
  695.7 4.5 all-to-all-start.7
  700.2 5.3 gather_fusion.3
  705.5 42.4 %all-to-all-done.7 = bf16[4,16,16,1024]{3,2,1,0:T(8,128)(2,1)} async-done(((bf16[4,16,16,1024]{3,2,1,0:T(8,128)(2,1)}), bf16[4,16,16,1024]{3,2,1,0:T(8,128)(2,1)}, u32[]{:S(2)}, u32[]{:S(2)}) %all-to-all-start.7) | async-done | bytes 2097184 | tf_op jit(solution)/shard_map/all_to_all | solution.py:99
  747.9 7.4 gather_fusion.6
  759.5 4.9 copy.61
  764.3 134.0 %reduce-scatter.3.cloned.1.call-done = bf16[16,256,768]{2,1,0:T(8,128)(2,1)} async-done(((bf16[16,1024,768]{2,1,0:T(8,128)(2,1)}), bf16[16,256,768]{2,1,0:T(8,128)(2,1)}) %reduce-scatter.3.cloned.1.call-update) | async-done | bytes 6291472 | tf_op jit(solution)/shard_map/reduce_scatter | solution.py:109
  (65 shorter events, 24.9 us)
Async XLA Ops:
  13.4 6.5 copy-start.6
  13.4 145.2 %all-to-all-start.2 = ((bf16[16,4,64,768]{3,2,0,1:T(8,128)(2,1)}), bf16[16,4,64,768]{3,2,0,1:T(8,128)(2,1)}, u32[]{:S(2)}, u32[]{:S(2)}) async-start(bf16[16,4,64,768]{3,2,0,1:T(8,128)(2,1)} %copy.47), calls=%async_computation.2 | async-start | bytes 12582912 | tf_op jit(solution)/shard_map/all_to_all | solution.py:17
  19.9 531.4 %all-gather.5.cloned.1.call-start = ((), (), s32[]{:S(2)}) async-start(), calls=%async_computation.11 | async-start | bytes 31457280 | tf_op jit(solution)/shard_map/all_gather | solution.py:59
  311.8 1.9 copy-start.1
  311.8 286.8 %all-gather.3.cloned.1.call-start = ((), (), s32[]{:S(2)}) async-start(), calls=%async_computation.10 | async-start | bytes 15728640 | tf_op jit(solution)/shard_map/all_gather | solution.py:60
  466.0 0.7 copy-start.4
  466.0 19.4 %copy-start.2 = (bf16[128,1024]{1,0:T(8,128)(2,1)S(1)}, bf16[128,1024]{1,0:T(8,128)(2,1)}, u32[]{:S(2)}) copy-start(bf16[128,1024]{1,0:T(8,128)(2,1)} %param.7) | copy-start | bytes 786436
  495.4 4.6 copy-start.5
  495.4 51.9 %all-to-all-start.4 = ((bf16[4,16,16,1024]{3,2,1,0:T(8,128)(2,1)}), bf16[4,16,16,1024]{3,2,1,0:T(8,128)(2,1)}, u32[]{:S(2)}, u32[]{:S(2)}) async-start(bf16[4,16,16,1024]{3,2,1,0:T(8,128)(2,1)} %bitcast.21), calls=%async_computation.4 | async-start | bytes 4194304 | tf_op jit(solution)/shard_map/all_to_all | solution.py:70
  500.2 6.2 copy-start.3
  547.3 51.3 %all-to-all-start.6 = ((bf16[4,16,16,1024]{3,2,1,0:T(8,128)(2,1)}), bf16[4,16,16,1024]{3,2,1,0:T(8,128)(2,1)S(1)}, u32[]{:S(2)}, u32[]{:S(2)}) async-start(bf16[4,16,16,1024]{3,2,1,0:T(8,128)(2,1)} %fusion.8), calls=%async_computation.6 | async-start | bytes 4194304 | tf_op jit(solution)/shard_map/all_to_all | solution.py:89
  551.0 208.4 %reduce-scatter.5.cloned.1.call-start = ((), (), s32[]{:S(2)}) async-start(), calls=%async_computation.13 | async-start | bytes 15728640 | tf_op jit(solution)/shard_map/reduce_scatter | solution.py:112
  616.7 1.1 copy-start.7
  616.7 281.6 %reduce-scatter.3.cloned.1.call-start = ((), (), s32[]{:S(2)}) async-start(), calls=%async_computation.12 | async-start | bytes 31457280 | tf_op jit(solution)/shard_map/reduce_scatter | solution.py:109
  643.7 51.9 %all-to-all-start.5 = ((bf16[4,16,16,1024]{3,2,1,0:T(8,128)(2,1)}), bf16[4,16,16,1024]{3,2,1,0:T(8,128)(2,1)S(1)}, u32[]{:S(2)}, u32[]{:S(2)}) async-start(bf16[4,16,16,1024]{3,2,1,0:T(8,128)(2,1)} %copy.55), calls=%async_computation.5 | async-start | bytes 4194304 | tf_op jit(solution)/shard_map/all_to_all | solution.py:82
  695.7 52.2 %all-to-all-start.7 = ((bf16[4,16,16,1024]{3,2,1,0:T(8,128)(2,1)}), bf16[4,16,16,1024]{3,2,1,0:T(8,128)(2,1)}, u32[]{:S(2)}, u32[]{:S(2)}) async-start(bf16[4,16,16,1024]{3,2,1,0:T(8,128)(2,1)} %copy.58), calls=%async_computation.7 | async-start | bytes 4194304 | tf_op jit(solution)/shard_map/all_to_all | solution.py:99
  755.3 2.1 copy-start
Sparse Core Ops, SparseCore 0:
  311.9 153.3 all-gather.4
  466.9 83.8 all-gather.2
  616.9 97.9 reduce-scatter.4
  717.9 180.4 reduce-scatter.2
where the time goes:
time: 906 us; the launch traced here: 905 us
  waiting for transfers between devices  414 us (46%)
  blocking collectives  286 us (32%)
  local copies, waits for them, and re-layouts  72.7 us (8%)
  matrix products  68.6 us (8%)
  other arithmetic  26.3 us (3%)
  starting transfers between devices  23.3 us (3%)
  between operations  14 us (2%)
    all_to_all x1, blocking collectives, relocate(): lax.all_to_all(pick_gu, 'expert', split_axis=1, concat_axis=1, tiled=True)  140 us
    all_to_all x1, waiting for transfers between devices, relocate(): lax.all_to_all(spread_gu, 'expert', split_axis=1, concat_axis=0, tiled=True)  136 us
    reduce_scatter x1, waiting for transfers between devices, shards(): lax.psum_scatter(part_gu.astype(jnp.bfloat16), 'dp', scatter_dimension=1,...  134 us
    all_to_all x1, blocking collectives, relocate(): lax.all_to_all(pick_dn, 'expert', split_axis=1, concat_axis=1, tiled=True)  72.7 us
    all_to_all x1, blocking collectives, relocate(): lax.all_to_all(spread_dn, 'expert', split_axis=1, concat_axis=0, tiled=True)  72.7 us
    all_to_all x1, waiting for transfers between devices, shards(): lax.all_to_all(d_rows, 'expert', split_axis=0, concat_axis=0, tiled=True)  42.4 us
    all_to_all x1, waiting for transfers between devices, shards(): lax.all_to_all(outgoing.reshape(row_shape), 'expert', split_axis=0, conca...  35 us
    all_to_all x1, waiting for transfers between devices, shards(): lax.all_to_all(scaled_cot.reshape(row_shape), 'expert', split_axis=0, con...  34.7 us
  transfers between devices with their start and end apart: 9, of which 6 were waited for; matrix products, arithmetic and copies ran while one was open for 14% of the time, Pallas kernels for 0%

commit v1 on v0

--- a/solution.py
+++ b/solution.py
@@ -46,7 +46,7 @@
     return (target_cell, source)
 
 
-def shards(tokens, expert_ids, gate_values, w_gate_up, w_down, new_slot, cotangent):
+def routed_shards(tokens, expert_ids, gate_values, w_gate_up, w_down, new_slot, cotangent):
     expert_peers = lax.axis_size("expert")
     home_slots = w_gate_up.shape[0]
     model_width = tokens.shape[1]
@@ -118,6 +118,141 @@
     return (layer_out, d_tokens, grad_gu, grad_dn)
 
 
+def cell_select(ids, gates, experts_here):
+    match = ids[..., None] == experts_here
+    member = jnp.any(match, axis=-2)
+    gate = jnp.sum(jnp.where(match, gates[..., None], 0.0), axis=-2)
+    count = ids.shape[-2]
+    below = (jnp.arange(count)[:, None] > jnp.arange(count)[None, :]).astype(jnp.bfloat16)
+    rank = jnp.einsum(
+        "tu,...uh->...th",
+        below,
+        member.astype(jnp.bfloat16),
+        preferred_element_type=jnp.float32,
+    ).astype(jnp.int32)
+    rank = jnp.where(member, rank, -1)
+    rank = jnp.swapaxes(rank, -1, -2)
+    gate = jnp.swapaxes(gate, -1, -2)
+    select = rank[..., None, :] == jnp.arange(MOST, dtype=jnp.int32)[:, None]
+    cell_gate = jnp.sum(jnp.where(select, gate[..., None, :], 0.0), axis=-1)
+    return select, cell_gate
+
+
+def pick_rows(spec, select, rows):
+    return jnp.einsum(
+        spec, select.astype(jnp.bfloat16), rows, preferred_element_type=jnp.float32
+    )
+
+
+def shared_shards(tokens, expert_ids, gate_values, w_gate_up, w_down, new_slot, cotangent):
+    expert_peers = lax.axis_size("expert")
+    dp_peers = lax.axis_size("dp")
+    me = lax.axis_index("expert")
+    home_slots = w_gate_up.shape[0]
+    model_width = tokens.shape[1]
+    hidden_width = w_down.shape[1]
+    token_count = tokens.shape[0]
+    share = model_width // dp_peers
+    here = me * home_slots + jnp.arange(home_slots, dtype=jnp.int32)
+
+    both = jnp.concatenate([tokens, cotangent], axis=1)
+    rows_all = lax.all_gather(both, "expert", axis=0, tiled=False)
+    ids_all = lax.all_gather(expert_ids, "expert", axis=0, tiled=False)
+    gates_all = lax.all_gather(gate_values, "expert", axis=0, tiled=False)
+    full_gu = lax.all_gather(w_gate_up, "dp", axis=1, tiled=True)
+    full_dn = lax.all_gather(w_down, "dp", axis=2, tiled=True)
+
+    select, cell_gate = cell_select(ids_all, gates_all, here)
+    cell_rows = pick_rows("shmt,std->hsmd", select, rows_all)
+    cell_gate = jnp.swapaxes(cell_gate, 0, 1)
+    cell_count = expert_peers * MOST
+    arrived = cell_rows[..., :model_width].astype(jnp.bfloat16)
+    arrived = arrived.reshape(home_slots, cell_count, model_width)
+    d_outputs = (cell_gate[..., None] * cell_rows[..., model_width:]).astype(jnp.bfloat16)
+    d_outputs = d_outputs.reshape(home_slots, cell_count, model_width)
+
+    gate_up = jnp.einsum("hrd,hdf->hrf", arrived, full_gu, preferred_element_type=jnp.float32)
+    d_act = jnp.einsum("hrd,hfd->hrf", d_outputs, full_dn, preferred_element_type=jnp.float32)
+    gate_part = gate_up[..., :hidden_width]
+    up_part = gate_up[..., hidden_width:]
+    sigmoid_g = jax.nn.sigmoid(gate_part)
+    silu_g = gate_part * sigmoid_g
+    activation = (silu_g * up_part).astype(jnp.bfloat16)
+    d_gate = d_act * up_part * sigmoid_g * (1.0 + gate_part * (1.0 - sigmoid_g))
+    d_up = d_act * silu_g
+    payload = jnp.concatenate(
+        [d_gate.astype(jnp.bfloat16), d_up.astype(jnp.bfloat16), activation], axis=-1
+    )
+    payload_all = lax.all_gather(payload, "expert", axis=0, tiled=True)
+
+    d_gate_up = payload[..., : 2 * hidden_width]
+    expert_out = jnp.einsum(
+        "hrf,hfd->hrd", activation, full_dn, preferred_element_type=jnp.float32
+    ).astype(jnp.bfloat16)
+    d_rows = jnp.einsum(
+        "hrf,hdf->hrd", d_gate_up, full_gu, preferred_element_type=jnp.float32
+    ).astype(jnp.bfloat16)
+    cells = (home_slots, expert_peers, MOST, model_width)
+    scaled_out = cell_gate[..., None] * expert_out.reshape(cells).astype(jnp.float32)
+    part_out = jnp.einsum(
+        "shmt,hsmd->std",
+        select.astype(jnp.float32),
+        scaled_out,
+        precision=lax.Precision.HIGHEST,
+        preferred_element_type=jnp.float32,
+    ).astype(jnp.bfloat16)
+    part_grad = pick_rows("shmt,hsmd->std", select, d_rows.reshape(cells)).astype(jnp.bfloat16)
+    back = lax.all_to_all(
+        jnp.concatenate([part_out, part_grad], axis=-1),
+        "expert",
+        split_axis=0,
+        concat_axis=0,
+        tiled=True,
+    )
+    summed = jnp.sum(back.astype(jnp.float32), axis=0).astype(jnp.bfloat16)
+    layer_out = summed[:, :model_width]
+    d_tokens = summed[:, model_width:]
+
+    wide = rows_all.reshape(expert_peers, token_count, 2, dp_peers, share)
+    wide = jnp.transpose(wide, (3, 0, 1, 2, 4))
+    narrow = lax.all_to_all(wide, "dp", split_axis=0, concat_axis=0, tiled=True)
+    narrow = narrow.reshape(dp_peers, expert_peers, token_count, 2 * share)
+    ids_group = lax.all_gather(ids_all, "dp", axis=0, tiled=False)
+    gates_group = lax.all_gather(gates_all, "dp", axis=0, tiled=False)
+    inverse = jnp.argsort(new_slot).astype(jnp.int32)
+    mine = lax.dynamic_slice_in_dim(inverse, me * home_slots, home_slots)
+    select_new, gate_new = cell_select(ids_group, gates_group, mine)
+    new_rows = pick_rows("pshmt,pstc->hpsmc", select_new, narrow)
+    gate_new = jnp.transpose(gate_new, (2, 0, 1, 3))
+    group_rows = dp_peers * cell_count
+    new_tokens = new_rows[..., :share].astype(jnp.bfloat16)
+    new_tokens = new_tokens.reshape(home_slots, group_rows, share)
+    new_douts = (gate_new[..., None] * new_rows[..., share:]).astype(jnp.bfloat16)
+    new_douts = new_douts.reshape(home_slots, group_rows, share)
+
+    mine_rows = payload_all[mine]
+    group_payload = lax.all_gather(mine_rows, "dp", axis=1, tiled=True)
+    grad_gu = jnp.einsum(
+        "hrc,hrf->hcf",
+        new_tokens,
+        group_payload[..., : 2 * hidden_width],
+        preferred_element_type=jnp.float32,
+    ).astype(jnp.bfloat16)
+    grad_dn = jnp.einsum(
+        "hrf,hrc->hfc",
+        group_payload[..., 2 * hidden_width :],
+        new_douts,
+        preferred_element_type=jnp.float32,
+    ).astype(jnp.bfloat16)
+    return (layer_out, d_tokens, grad_gu, grad_dn)
+
+
+def shards(tokens, expert_ids, *rest):
+    if lax.axis_size("expert") < expert_ids.shape[1]:
+        return shared_shards(tokens, expert_ids, *rest)
+    return routed_shards(tokens, expert_ids, *rest)
+
+
 def solution(mesh):
     return jax.shard_map(
         shards,

time: 906 us -> 620 us (0.68)
  blocking collectives: 286 us -> 39.7 us
  local copies, waits for them, and re-layouts: 72.7 us -> 22.4 us
  waiting for transfers between devices: 414 us -> 458 us
  other arithmetic: 26.3 us -> 11.8 us
  starting transfers between devices: 23.3 us -> 9.28 us
    all_gather x2 -> x5, waiting for transfers between devices: 0.02 us -> 404 us  [the longest x1 164 us: shared_shards(): payload_all = lax.all_gather(payload, 'expert', axis=0, tiled=True)]
    all_to_all x3 -> x0, blocking collectives: 286 us -> none  [the longest x1 140 us: relocate(): lax.all_to_all(pick_gu, 'expert', split_axis=1, concat_axis=1, tiled=True)]
    all_to_all x5 -> x2, waiting for transfers between devices: 280 us -> 52.6 us  [the longest x1 28.2 us: shared_shards(): lax.all_to_all(jnp.concatenate([part_out, part_grad], axis=-1), 'expert',...]
    reduce_scatter x2 -> x0, waiting for transfers between devices: 134 us -> none  [the longest x1 134 us: shards(): lax.psum_scatter(part_gu.astype(jnp.bfloat16), 'dp', scatter_dimension=1,...]
    all_gather x0 -> x4, blocking collectives: none -> 39.7 us  [the longest x1 14.9 us: shared_shards(): ids_all = lax.all_gather(expert_ids, 'expert', axis=0, tiled=False)]
    gather x9 -> x1, local copies, waits for them, and re-layouts: 42.4 us -> 5.89 us  [shared_shards(): mine_rows = payload_all[mine]]
    another operation x3 -> x0, other arithmetic: 18.2 us -> none
    all_to_all x5 -> x2, starting transfers between devices: 23 us -> 8.9 us  [the longest x1 4.46 us: shared_shards(): narrow = lax.all_to_all(wide, 'dp', split_axis=0, concat_axis=0, tiled=True)]
  transfers between devices with their start and end apart: 9 -> 7, of which waited for: 6 -> 6; matrix products, arithmetic and copies ran while one was open for 14% -> 10% of each run, Pallas kernels for 0% -> 0%
where the time goes in v1:
time: 620 us; the launch traced here: 619 us
  waiting for transfers between devices  458 us (74%)
  matrix products  63.8 us (10%)
  blocking collectives  39.7 us (6%)
  local copies, waits for them, and re-layouts  22.4 us (4%)
  between operations  14 us (2%)
  other arithmetic  11.8 us (2%)
  starting transfers between devices  9.28 us (1%)
    all_gather x1, waiting for transfers between devices, shared_shards(): payload_all = lax.all_gather(payload, 'expert', axis=0, tiled=True)  164 us
    all_gather x1, waiting for transfers between devices, shared_shards(): full_gu = lax.all_gather(w_gate_up, 'dp', axis=1, tiled=True)  150 us
    all_gather x1, waiting for transfers between devices, shared_shards(): full_dn = lax.all_gather(w_down, 'dp', axis=2, tiled=True)  70.8 us
    all_to_all x1, waiting for transfers between devices, shared_shards(): lax.all_to_all(jnp.concatenate([part_out, part_grad], axis=-1), 'expert',...  28.2 us
    all_to_all x1, waiting for transfers between devices, shared_shards(): narrow = lax.all_to_all(wide, 'dp', split_axis=0, concat_axis=0, tiled=True)  24.4 us
    all_gather x1, waiting for transfers between devices, shared_shards(): rows_all = lax.all_gather(both, 'expert', axis=0, tiled=False)  19.6 us
    all_gather x1, blocking collectives, shared_shards(): ids_all = lax.all_gather(expert_ids, 'expert', axis=0, tiled=False)  14.9 us
    dot_general x1, matrix products, shared_shards(): jnp.einsum('hrd,hdf->hrf', arrived, full_gu, preferred_element_type=jnp.f...  14.5 us
  transfers between devices with their start and end apart: 7, of which 6 were waited for; matrix products, arithmetic and copies ran while one was open for 10% of the time, Pallas kernels for 0%

profile of v1, /device:TPU:0, one launch (start us, length us, event | category | flops | bytes accessed | tf_op | source)
XLA Modules:
  0.0 619.2 jit_solution(7019774872820202553)
XLA Ops:
  7.2 1.9 pad_maximum_fusion.2
  10.7 14.9 %all-gather = s32[512,8]{0,1:T(8,128)S(1)} all-gather(s32[128,8]{0,1:T(8,128)S(1)} %copy-done.3), channel_id=2, replica_groups=mesh['groups'=2,'expert'=4,'dp'=4] {'expert'}, dimensions={0}, use_global_device_ids=true | all-gather | bytes 20480 | tf_op jit(solution)/shard_map/all_gather | solution.py:160
  25.6 13.5 %all-gather.1 = f32[512,8]{0,1:T(8,128)S(1)} all-gather(f32[128,8]{0,1:T(8,128)S(1)} %copy-done.4), channel_id=3, replica_groups=mesh['groups'=2,'expert'=4,'dp'=4] {'expert'}, dimensions={0}, use_global_device_ids=true | all-gather | bytes 20480 | tf_op jit(solution)/shard_map/all_gather | solution.py:161
  39.7 19.6 %all-gather.18.cloned.1.call-done = bf16[512,2048]{1,0:T(8,128)(2,1)} async-done(((bf16[128,2048]{1,0:T(8,128)(2,1)}), bf16[512,2048]{1,0:T(8,128)(2,1)}) %all-gather.18.cloned.1.call-update) | async-done | bytes 2097168 | tf_op jit(solution)/shard_map/all_gather | solution.py:159
  59.3 2.8 convolution_bitcast_fusion
  62.9 1.6 copy.46
  64.6 149.6 %all-gather.12.cloned.1.call-done = bf16[16,1024,768]{2,1,0:T(8,128)(2,1)} async-done(((bf16[16,256,768]{2,1,0:T(8,128)(2,1)}), bf16[16,1024,768]{2,1,0:T(8,128)(2,1)}) %all-gather.12.cloned.1.call-update) | async-done | bytes 25165840 | tf_op jit(solution)/shard_map/all_gather | solution.py:162
  214.1 14.5 %fusion.37 = f32[16,64,768]{2,1,0:T(8,128)} fusion(bf16[16,64,1024]{2,1,0:T(8,128)(2,1)S(1)} %bitcast.63, bf16[16,1024,768]{2,1,0:T(8,128)(2,1)} %all-gather.12.cloned.1.call-done), kind=kOutput, calls=%fused_computation.63 | convolution fusion | flops 1610612736 | bytes 30408704 | tf_op jit(solution)/shard_map/hrd,hdf->hrf/dot_general | solution.py:174
  228.7 70.8 %all-gather.14.cloned.1.call-done = bf16[16,384,1024]{2,1,0:T(8,128)(2,1)} async-done(((bf16[16,384,256]{2,1,0:T(8,128)(2,1)}), bf16[16,384,1024]{2,1,0:T(8,128)(2,1)}) %all-gather.14.cloned.1.call-update) | async-done | bytes 12582928 | tf_op jit(solution)/shard_map/all_gather | solution.py:163
  299.5 10.1 %multiply_convert_fusion.1 = (bf16[16,64,384]{2,1,0:T(8,128)(2,1)S(1)}, bf16[16,64,384]{2,1,0:T(8,128)(2,1)S(1)}, bf16[16,64,384]{2,1,0:T(8,128)(2,1)S(1)}) fusion(f32[16,64,768]{2,1,0:T(8,128)} %fusion.37, bf16[16,64,1024]{2,1,0:T(8,128)(2,1)} %bitcast.66, bf16[16,384,1024]{2,1,0:T(8,128)(2,1)} %all-gather.14.cloned.1.call-done), kind=kOutput, calls=%fused_computation.34 | convolution fusion | flops 811204608 | bytes 20185088 | tf_op jit(solution)/shard_map/hrd,hfd->hrf/dot_general | solution.py:175
  310.8 1.7 pad_maximum_fusion
  313.2 2.0 sort.17
  315.3 164.2 %all-gather.16.cloned.1.call-done = bf16[64,64,1152]{2,1,0:T(8,128)(2,1)} async-done(((bf16[16,64,1152]{2,1,0:T(8,128)(2,1)}), bf16[64,64,1152]{2,1,0:T(8,128)(2,1)}) %all-gather.16.cloned.1.call-update) | async-done | bytes 9437200 | tf_op jit(solution)/shard_map/all_gather | solution.py:186
  479.5 5.9 gather_fusion
  485.4 3.3 reshape.50
  488.7 3.2 copy.69
  491.9 4.5 all-to-all-start.1
  496.4 13.1 %convolution_convert_fusion = bf16[16,64,1024]{2,1,0:T(8,128)(2,1)S(1)} fusion(bf16[16,1024,768]{2,1,0:T(8,128)(2,1)} %all-gather.12.cloned.1.call-done, bf16[16,64,384]{2,1,0:T(8,128)(2,1)} %copy-done.2, bf16[16,64,384]{2,1,0:T(8,128)(2,1)} %copy-done.1), kind=kOutput, calls=%fused_computation.28 | convolution fusion | flops 1614807040 | bytes 28835840 | tf_op jit(solution)/shard_map/hrf,hdf->hrd/dot_general | solution.py:192
  509.9 6.9 %convolution_convert_fusion.1 = bf16[16,64,1024]{2,1,0:T(8,128)(2,1)S(1)} fusion(bf16[16,64,384]{2,1,0:T(8,128)(2,1)S(1)} %get-tuple-element.10, bf16[16,384,1024]{2,1,0:T(8,128)(2,1)} %all-gather.14.cloned.1.call-done), kind=kOutput, calls=%fused_computation.29 | convolution fusion | flops 806354944 | bytes 15466496 | tf_op jit(solution)/shard_map/hrf,hfd->hrd/dot_general | solution.py:189
  516.9 2.2 bitcast_convert_fusion.1
  519.1 1.5 pad_maximum_fusion.1
  520.5 24.4 %all-to-all-done.1 = bf16[4,4,128,2,256]{4,3,2,1,0:T(2,128)(2,1)} async-done(((bf16[4,4,128,2,256]{4,3,2,1,0:T(2,128)(2,1)}), bf16[4,4,128,2,256]{4,3,2,1,0:T(2,128)(2,1)}, u32[]{:S(2)}, u32[]{:S(2)}) %all-to-all-start.1) | async-done | bytes 2097184 | tf_op jit(solution)/shard_map/all_to_all | solution.py:218
  544.9 4.4 all-to-all-start
  549.4 5.6 all-gather.3
  555.0 5.8 all-gather.5
  562.0 3.2 reshape.76
  565.2 1.2 convolution_bitcast_fusion.1
  567.8 1.6 copy.51
  569.4 28.2 %all-to-all-done = bf16[4,128,2048]{2,1,0:T(8,128)(2,1)} async-done(((bf16[4,128,2048]{2,1,0:T(8,128)(2,1)}), bf16[4,128,2048]{2,1,0:T(8,128)(2,1)}, u32[]{:S(2)}, u32[]{:S(2)}) %all-to-all-start) | async-done | bytes 2097184 | tf_op jit(solution)/shard_map/all_to_all | solution.py:205
  597.7 2.0 reduce_sum.50
  600.5 7.5 %fusion.5 = bf16[16,256,768]{2,1,0:T(8,128)(2,1)} fusion(bf16[16,256,256]{2,1,0:T(8,128)(2,1)S(1)} %bitcast.61, bf16[16,256,1152]{2,1,0:T(8,128)(2,1)} %all-gather.20.cloned.1.call-done), kind=kOutput, calls=%fused_computation.12 | convolution fusion | flops 1613758464 | bytes 14680064 | tf_op jit(solution)/shard_map/hrc,hrf->hcf/dot_general | solution.py:235
  608.0 4.7 fusion.10
  (43 shorter events, 8.8 us)
Async XLA Ops:
  7.2 52.1 %all-gather.18.cloned.1.call-start = ((), (), s32[]{:S(2)}) async-start(), calls=%async_computation.5 | async-start | bytes 2621440 | tf_op jit(solution)/shard_map/all_gather | solution.py:159
  9.1 205.0 %all-gather.12.cloned.1.call-start = ((), (), s32[]{:S(2)}) async-start(), calls=%async_computation.2 | async-start | bytes 31457280 | tf_op jit(solution)/shard_map/all_gather | solution.py:162
  9.9 0.8 copy-start.3
  9.9 15.7 %copy-start.4 = (f32[128,8]{0,1:T(8,128)S(1)}, f32[128,8]{0,1:T(8,128)}, u32[]{:S(2)}) copy-start(f32[128,8]{0,1:T(8,128)} %param.9) | copy-start | bytes 12292
  9.9 289.7 %all-gather.14.cloned.1.call-start = ((), (), s32[]{:S(2)}) async-start(), calls=%async_computation.3 | async-start | bytes 15728640 | tf_op jit(solution)/shard_map/all_gather | solution.py:163
  10.6 468.9 %all-gather.16.cloned.1.call-start = ((), (), s32[]{:S(2)}) async-start(), calls=%async_computation.4 | async-start | bytes 11796480 | tf_op jit(solution)/shard_map/all_gather | solution.py:186
  309.6 0.9 copy-start.1
  309.7 1.1 copy-start.2
  312.5 0.7 copy-start.5
  312.5 288.0 %all-gather.20.cloned.1.call-start = ((), (), s32[]{:S(2)}) async-start(), calls=%async_computation.6 | async-start | bytes 11796480 | tf_op jit(solution)/shard_map/all_gather | solution.py:234
  491.9 53.0 %all-to-all-start.1 = ((bf16[4,4,128,2,256]{4,3,2,1,0:T(2,128)(2,1)}), bf16[4,4,128,2,256]{4,3,2,1,0:T(2,128)(2,1)}, u32[]{:S(2)}, u32[]{:S(2)}) async-start(bf16[4,4,128,2,256]{4,3,2,1,0:T(2,128)(2,1)} %bitcast.59), calls=%async_computation.1 | async-start | bytes 4194304 | tf_op jit(solution)/shard_map/all_to_all | solution.py:218
  544.9 52.7 %all-to-all-start = ((bf16[4,128,2048]{2,1,0:T(8,128)(2,1)}), bf16[4,128,2048]{2,1,0:T(8,128)(2,1)}, u32[]{:S(2)}, u32[]{:S(2)}) async-start(bf16[4,128,2048]{2,1,0:T(8,128)(2,1)} %pad_maximum_fusion.1), calls=%async_computation | async-start | bytes 4194304 | tf_op jit(solution)/shard_map/all_to_all | solution.py:205
  600.5 7.5 %copy-start = (bf16[16,4,4,16,256]{4,3,2,1,0:T(8,128)(2,1)S(1)}, bf16[16,4,4,16,256]{4,3,2,1,0:T(8,128)(2,1)}, u32[]{:S(2)}) copy-start(bf16[16,4,4,16,256]{4,3,2,1,0:T(8,128)(2,1)} %copy.51) | copy-start | bytes 6291460
Sparse Core Ops, SparseCore 0:
  10.1 49.0 all-gather.17
  60.8 153.2 all-gather.11
  215.7 83.7 all-gather.13
  312.6 166.7 all-gather.15
  485.5 85.5 all-gather.19

commit v2 on v1

--- a/solution.py
+++ b/solution.py
@@ -171,6 +171,26 @@
     d_outputs = (cell_gate[..., None] * cell_rows[..., model_width:]).astype(jnp.bfloat16)
     d_outputs = d_outputs.reshape(home_slots, cell_count, model_width)
 
+    inverse = jnp.argsort(new_slot).astype(jnp.int32)
+    wide = rows_all.reshape(expert_peers, token_count, 2, dp_peers, share)
+    wide = jnp.transpose(wide, (3, 0, 1, 2, 4))
+    narrow = lax.all_to_all(wide, "dp", split_axis=0, concat_axis=0, tiled=True)
+    narrow = narrow.reshape(dp_peers, expert_peers, token_count, 2 * share)
+    ids_group = lax.all_gather(ids_all, "dp", axis=0, tiled=False)
+    gates_group = lax.all_gather(gates_all, "dp", axis=0, tiled=False)
+    mine = lax.dynamic_slice_in_dim(inverse, me * home_slots, home_slots)
+    select_new, gate_new = cell_select(ids_group, gates_group, mine)
+    new_rows = pick_rows("pshmt,pstc->hpsmc", select_new, narrow)
+    gate_new = jnp.transpose(gate_new, (2, 0, 1, 3))
+    group_rows = dp_peers * cell_count
+    new_tokens = new_rows[..., :share].astype(jnp.bfloat16)
+    new_tokens = new_tokens.reshape(home_slots, group_rows, share)
+    new_douts = (gate_new[..., None] * new_rows[..., share:]).astype(jnp.bfloat16)
+    new_douts = new_douts.reshape(home_slots, group_rows, share)
+    arrived, d_outputs, new_tokens, new_douts = lax.optimization_barrier(
+        (arrived, d_outputs, new_tokens, new_douts)
+    )
+
     gate_up = jnp.einsum("hrd,hdf->hrf", arrived, full_gu, preferred_element_type=jnp.float32)
     d_act = jnp.einsum("hrd,hfd->hrf", d_outputs, full_dn, preferred_element_type=jnp.float32)
     gate_part = gate_up[..., :hidden_width]
@@ -183,7 +203,15 @@
     payload = jnp.concatenate(
         [d_gate.astype(jnp.bfloat16), d_up.astype(jnp.bfloat16), activation], axis=-1
     )
-    payload_all = lax.all_gather(payload, "expert", axis=0, tiled=True)
+    pay_shape = (home_slots, expert_peers, MOST, 3 * hidden_width)
+    spread = jnp.transpose(payload.reshape(pay_shape), (1, 0, 2, 3))
+    spread = lax.all_to_all(spread, "expert", split_axis=0, concat_axis=0, tiled=True)
+    spread = spread.reshape(expert_peers * home_slots, MOST, 3 * hidden_width)
+    spread = spread[inverse.reshape(expert_peers, home_slots)]
+    spread = lax.all_to_all(spread, "expert", split_axis=0, concat_axis=0, tiled=True)
+    mine_rows = jnp.transpose(spread, (1, 0, 2, 3)).reshape(
+        home_slots, cell_count, 3 * hidden_width
+    )
 
     d_gate_up = payload[..., : 2 * hidden_width]
     expert_out = jnp.einsum(
@@ -202,8 +230,10 @@
         preferred_element_type=jnp.float32,
     ).astype(jnp.bfloat16)
     part_grad = pick_rows("shmt,hsmd->std", select, d_rows.reshape(cells)).astype(jnp.bfloat16)
+    sent = jnp.concatenate([part_out, part_grad], axis=-1)
+    sent, mine_rows = lax.optimization_barrier((sent, mine_rows))
     back = lax.all_to_all(
-        jnp.concatenate([part_out, part_grad], axis=-1),
+        sent,
         "expert",
         split_axis=0,
         concat_axis=0,
@@ -213,24 +243,6 @@
     layer_out = summed[:, :model_width]
     d_tokens = summed[:, model_width:]
 
-    wide = rows_all.reshape(expert_peers, token_count, 2, dp_peers, share)
-    wide = jnp.transpose(wide, (3, 0, 1, 2, 4))
-    narrow = lax.all_to_all(wide, "dp", split_axis=0, concat_axis=0, tiled=True)
-    narrow = narrow.reshape(dp_peers, expert_peers, token_count, 2 * share)
-    ids_group = lax.all_gather(ids_all, "dp", axis=0, tiled=False)
-    gates_group = lax.all_gather(gates_all, "dp", axis=0, tiled=False)
-    inverse = jnp.argsort(new_slot).astype(jnp.int32)
-    mine = lax.dynamic_slice_in_dim(inverse, me * home_slots, home_slots)
-    select_new, gate_new = cell_select(ids_group, gates_group, mine)
-    new_rows = pick_rows("pshmt,pstc->hpsmc", select_new, narrow)
-    gate_new = jnp.transpose(gate_new, (2, 0, 1, 3))
-    group_rows = dp_peers * cell_count
-    new_tokens = new_rows[..., :share].astype(jnp.bfloat16)
-    new_tokens = new_tokens.reshape(home_slots, group_rows, share)
-    new_douts = (gate_new[..., None] * new_rows[..., share:]).astype(jnp.bfloat16)
-    new_douts = new_douts.reshape(home_slots, group_rows, share)
-
-    mine_rows = payload_all[mine]
     group_payload = lax.all_gather(mine_rows, "dp", axis=1, tiled=True)
     grad_gu = jnp.einsum(
         "hrc,hrf->hcf",

time: 620 us -> 534 us (0.86)
  waiting for transfers between devices: 458 us -> 314 us
  blocking collectives: 39.7 us -> 89.6 us
    all_gather x1 -> x0, waiting for transfers between devices: 164 us -> none  [shared_shards(): payload_all = lax.all_gather(payload, 'expert', axis=0, tiled=True)]
    all_to_all x1 -> x2, waiting for transfers between devices: 28.2 us -> 84.6 us  [shared_shards(): lax.all_to_all(spread, 'expert', split_axis=0, concat_axis=0, tiled=True)]
    all_to_all x0 -> x1, blocking collectives: none -> 50.9 us  [shared_shards(): lax.all_to_all(sent, 'expert', split_axis=0, concat_axis=0, tiled=True)]
    all_gather x1, waiting for transfers between devices: 150 us -> 109 us  [shared_shards(): full_gu = lax.all_gather(w_gate_up, 'dp', axis=1, tiled=True)]
    all_gather x1, waiting for transfers between devices: 19.6 us -> 7.27 us  [shared_shards(): rows_all = lax.all_gather(both, 'expert', axis=0, tiled=False)]
    all_to_all x1, waiting for transfers between devices: 24.4 us -> 35.9 us  [shared_shards(): narrow = lax.all_to_all(wide, 'dp', split_axis=0, concat_axis=0, tiled=True)]
    all_gather x1, waiting for transfers between devices: 0.01 us -> 8.76 us  [shared_shards(): group_payload = lax.all_gather(mine_rows, 'dp', axis=1, tiled=True)]
  transfers between devices with their start and end apart: 7 -> 7, of which waited for: 6 -> 7; matrix products, arithmetic and copies ran while one was open for 10% -> 13% of each run, Pallas kernels for 0% -> 0%
where the time goes in v2:
time: 534 us; the launch traced here: 533 us
  waiting for transfers between devices  314 us (59%)
  blocking collectives  89.6 us (17%)
  matrix products  67.6 us (13%)
  local copies, waits for them, and re-layouts  25.3 us (5%)
  between operations  14 us (3%)
  starting transfers between devices  13 us (2%)
  other arithmetic  9.14 us (2%)
    all_gather x1, waiting for transfers between devices, shared_shards(): full_gu = lax.all_gather(w_gate_up, 'dp', axis=1, tiled=True)  109 us
    all_to_all x2, waiting for transfers between devices, shared_shards(): lax.all_to_all(spread, 'expert', split_axis=0, concat_axis=0, tiled=True)  84.6 us
    all_gather x1, waiting for transfers between devices, shared_shards(): full_dn = lax.all_gather(w_down, 'dp', axis=2, tiled=True)  67.6 us
    all_to_all x1, blocking collectives, shared_shards(): lax.all_to_all(sent, 'expert', split_axis=0, concat_axis=0, tiled=True)  50.9 us
    all_to_all x1, waiting for transfers between devices, shared_shards(): narrow = lax.all_to_all(wide, 'dp', split_axis=0, concat_axis=0, tiled=True)  35.9 us
    dot_general x1, matrix products, shared_shards(): jnp.einsum('hrd,hdf->hrf', arrived, full_gu, preferred_element_type=jnp.f...  15.6 us
    all_gather x1, blocking collectives, shared_shards(): ids_all = lax.all_gather(expert_ids, 'expert', axis=0, tiled=False)  14.9 us
    all_gather x1, blocking collectives, shared_shards(): gates_all = lax.all_gather(gate_values, 'expert', axis=0, tiled=False)  13.4 us
  transfers between devices with their start and end apart: 7, of which 7 were waited for; matrix products, arithmetic and copies ran while one was open for 13% of the time, Pallas kernels for 0%

profile of v2, /device:TPU:0, one launch (start us, length us, event | category | flops | bytes accessed | tf_op | source)
XLA Modules:
  0.0 532.8 jit_solution(5919196372204041554)
XLA Ops:
  7.2 1.9 pad_maximum_fusion.2
  10.6 2.0 sort.17
  12.8 14.9 %all-gather = s32[512,8]{0,1:T(8,128)S(1)} all-gather(s32[128,8]{0,1:T(8,128)S(1)} %copy-done.4), channel_id=2, replica_groups=mesh['groups'=2,'expert'=4,'dp'=4] {'expert'}, dimensions={0}, use_global_device_ids=true | all-gather | bytes 20480 | tf_op jit(solution)/shard_map/all_gather | solution.py:160
  27.7 13.4 %all-gather.1 = f32[512,8]{0,1:T(8,128)S(1)} all-gather(f32[128,8]{0,1:T(8,128)S(1)} %copy-done.5), channel_id=3, replica_groups=mesh['groups'=2,'expert'=4,'dp'=4] {'expert'}, dimensions={0}, use_global_device_ids=true | all-gather | bytes 20480 | tf_op jit(solution)/shard_map/all_gather | solution.py:161
  41.0 5.2 all-gather.3
  46.3 5.2 all-gather.4
  52.0 7.3 %all-gather.16.cloned.1.call-done = bf16[512,2048]{1,0:T(8,128)(2,1)} async-done(((bf16[128,2048]{1,0:T(8,128)(2,1)}), bf16[512,2048]{1,0:T(8,128)(2,1)}) %all-gather.16.cloned.1.call-update) | async-done | bytes 2097168 | tf_op jit(solution)/shard_map/all_gather | solution.py:159
  59.3 3.3 reshape.89
  62.6 3.2 copy.77
  65.8 3.8 all-to-all-start
  70.9 3.4 convolution_bitcast_fusion
  78.1 35.9 %all-to-all-done = bf16[4,4,128,2,256]{4,3,2,1,0:T(2,128)(2,1)S(1)} async-done(((bf16[4,4,128,2,256]{4,3,2,1,0:T(2,128)(2,1)}), bf16[4,4,128,2,256]{4,3,2,1,0:T(2,128)(2,1)S(1)}, u32[]{:S(2)}, u32[]{:S(2)}) %all-to-all-start) | async-done | bytes 2097184 | tf_op jit(solution)/shard_map/all_to_all | solution.py:177
  114.0 2.6 reshape.117
  116.6 2.8 convolution_bitcast_fusion.1
  124.1 108.6 %all-gather.10.cloned.1.call-done = bf16[16,1024,768]{2,1,0:T(8,128)(2,1)} async-done(((bf16[16,256,768]{2,1,0:T(8,128)(2,1)}), bf16[16,1024,768]{2,1,0:T(8,128)(2,1)}) %all-gather.10.cloned.1.call-update) | async-done | bytes 25165840 | tf_op jit(solution)/shard_map/all_gather | solution.py:162
  232.6 15.6 %fusion.37 = f32[16,64,768]{2,1,0:T(8,128)} fusion(bf16[16,64,1024]{2,1,0:T(8,128)(2,1)S(1)} %bitcast.78, bf16[16,1024,768]{2,1,0:T(8,128)(2,1)} %all-gather.10.cloned.1.call-done), kind=kOutput, calls=%fused_computation.64 | convolution fusion | flops 1610612736 | bytes 30408704 | tf_op jit(solution)/shard_map/hrd,hdf->hrf/dot_general | solution.py:194
  248.3 67.6 %all-gather.12.cloned.1.call-done = bf16[16,384,1024]{2,1,0:T(8,128)(2,1)} async-done(((bf16[16,384,256]{2,1,0:T(8,128)(2,1)}), bf16[16,384,1024]{2,1,0:T(8,128)(2,1)}) %all-gather.12.cloned.1.call-update) | async-done | bytes 12582928 | tf_op jit(solution)/shard_map/all_gather | solution.py:163
  315.9 10.1 %multiply_convert_fusion.1 = (bf16[16,64,384]{2,1,0:T(8,128)(2,1)S(1)}, bf16[16,64,384]{2,1,0:T(8,128)(2,1)S(1)}, bf16[16,64,384]{2,1,0:T(8,128)(2,1)S(1)}) fusion(f32[16,64,768]{2,1,0:T(8,128)} %fusion.37, bf16[16,64,1024]{2,1,0:T(8,128)(2,1)} %bitcast.81, bf16[16,384,1024]{2,1,0:T(8,128)(2,1)} %all-gather.12.cloned.1.call-done), kind=kOutput, calls=%fused_computation.35 | convolution fusion | flops 811204608 | bytes 20185088 | tf_op jit(solution)/shard_map/hrd,hfd->hrf/dot_general | solution.py:195
  328.7 4.6 all-to-all-start.1
  333.5 54.1 %all-to-all-done.1 = bf16[4,16,16,1152]{3,2,1,0:T(8,128)(2,1)S(1)} async-done(((bf16[4,16,16,1152]{3,2,1,0:T(8,128)(2,1)}), bf16[4,16,16,1152]{3,2,1,0:T(8,128)(2,1)S(1)}, u32[]{:S(2)}, u32[]{:S(2)}) %all-to-all-start.1) | async-done | bytes 2359328 | tf_op jit(solution)/shard_map/all_to_all | solution.py:208
  387.5 2.2 gather_fusion
  389.7 4.5 all-to-all-start.2
  394.3 13.1 %convolution_convert_fusion = bf16[16,64,1024]{2,1,0:T(8,128)(2,1)S(1)} fusion(bf16[16,1024,768]{2,1,0:T(8,128)(2,1)} %all-gather.10.cloned.1.call-done, bf16[16,64,384]{2,1,0:T(8,128)(2,1)} %copy-done.3, bf16[16,64,384]{2,1,0:T(8,128)(2,1)} %copy-done.2), kind=kOutput, calls=%fused_computation.29 | convolution fusion | flops 1614807040 | bytes 28835840 | tf_op jit(solution)/shard_map/hrf,hdf->hrd/dot_general | solution.py:220
  407.9 6.9 %convolution_convert_fusion.1 = bf16[16,64,1024]{2,1,0:T(8,128)(2,1)S(1)} fusion(bf16[16,64,384]{2,1,0:T(8,128)(2,1)S(1)} %get-tuple-element.20, bf16[16,384,1024]{2,1,0:T(8,128)(2,1)} %all-gather.12.cloned.1.call-done), kind=kOutput, calls=%fused_computation.30 | convolution fusion | flops 806354944 | bytes 15466496 | tf_op jit(solution)/shard_map/hrf,hfd->hrd/dot_general | solution.py:217
  414.8 2.2 bitcast_convert_fusion.1
  417.2 30.5 %all-to-all-done.2 = bf16[4,16,16,1152]{3,2,1,0:T(8,128)(2,1)} async-done(((bf16[4,16,16,1152]{3,2,1,0:T(8,128)(2,1)}), bf16[4,16,16,1152]{3,2,1,0:T(8,128)(2,1)}, u32[]{:S(2)}, u32[]{:S(2)}) %all-to-all-start.2) | async-done | bytes 2359328 | tf_op jit(solution)/shard_map/all_to_all | solution.py:211
  447.7 3.3 copy.56
  451.1 50.9 %all_to_all.20 = bf16[4,128,2048]{2,1,0:T(8,128)(2,1)} all-to-all(bf16[4,128,2048]{2,1,0:T(8,128)(2,1)S(1)} %pad_maximum_fusion.1), channel_id=1, replica_groups=mesh['groups'=2,'expert'=4,'dp'=4] {'expert'}, dimensions={0} | all-to-all | bytes 4194304 | tf_op jit(solution)/shard_map/all_to_all | solution.py:235
  502.0 2.0 reduce_sum.52
  504.9 8.8 %all-gather.14.cloned.1.call-done = bf16[16,256,1152]{2,1,0:T(8,128)(2,1)} async-done(((bf16[16,64,1152]{2,1,0:T(8,128)(2,1)}), bf16[16,256,1152]{2,1,0:T(8,128)(2,1)}) %all-gather.14.cloned.1.call-update) | async-done | bytes 9437200 | tf_op jit(solution)/shard_map/all_gather | solution.py:246
  513.6 5.3 fusion.10
  518.9 7.3 %fusion.5 = bf16[16,256,768]{2,1,0:T(8,128)(2,1)} fusion(bf16[16,256,256]{2,1,0:T(8,128)(2,1)S(1)} %bitcast.75, bf16[16,256,1152]{2,1,0:T(8,128)(2,1)} %all-gather.14.cloned.1.call-done), kind=kOutput, calls=%fused_computation.12 | convolution fusion | flops 1613758464 | bytes 14680064 | tf_op jit(solution)/shard_map/hrc,hrf->hcf/dot_general | solution.py:247
  (50 shorter events, 16.2 us)
Async XLA Ops:
  7.2 52.1 %all-gather.16.cloned.1.call-start = ((), (), s32[]{:S(2)}) async-start(), calls=%async_computation.7 | async-start | bytes 2621440 | tf_op jit(solution)/shard_map/all_gather | solution.py:159
  9.1 223.5 %all-gather.10.cloned.1.call-start = ((), (), s32[]{:S(2)}) async-start(), calls=%async_computation.4 | async-start | bytes 31457280 | tf_op jit(solution)/shard_map/all_gather | solution.py:162
  9.9 0.8 copy-start.6
  9.9 2.9 copy-start.4
  9.9 17.8 %copy-start.5 = (f32[128,8]{0,1:T(8,128)S(1)}, f32[128,8]{0,1:T(8,128)}, u32[]{:S(2)}) copy-start(f32[128,8]{0,1:T(8,128)} %param.9) | copy-start | bytes 12292
  9.9 306.0 %all-gather.12.cloned.1.call-start = ((), (), s32[]{:S(2)}) async-start(), calls=%async_computation.5 | async-start | bytes 15728640 | tf_op jit(solution)/shard_map/all_gather | solution.py:163
  65.8 48.2 %all-to-all-start = ((bf16[4,4,128,2,256]{4,3,2,1,0:T(2,128)(2,1)}), bf16[4,4,128,2,256]{4,3,2,1,0:T(2,128)(2,1)S(1)}, u32[]{:S(2)}, u32[]{:S(2)}) async-start(bf16[4,4,128,2,256]{4,3,2,1,0:T(2,128)(2,1)} %bitcast.76), calls=%async_computation | async-start | bytes 4194304 | tf_op jit(solution)/shard_map/all_to_all | solution.py:177
  122.4 110.2 %copy-start.1 = (bf16[16,4,16,1024]{3,2,1,0:T(8,128)(2,1)S(1)}, bf16[16,4,16,1024]{3,2,1,0:T(8,128)(2,1)}, u32[]{:S(2)}) copy-start(bf16[16,4,16,1024]{3,2,1,0:T(8,128)(2,1)} %copy.48) | copy-start | bytes 6291460
  326.0 0.9 copy-start.2
  326.0 1.1 copy-start.3
  328.7 58.8 %all-to-all-start.1 = ((bf16[4,16,16,1152]{3,2,1,0:T(8,128)(2,1)}), bf16[4,16,16,1152]{3,2,1,0:T(8,128)(2,1)S(1)}, u32[]{:S(2)}, u32[]{:S(2)}) async-start(bf16[4,16,16,1152]{3,2,1,0:T(8,128)(2,1)} %bitcast.73), calls=%async_computation.1 | async-start | bytes 4718592 | tf_op jit(solution)/shard_map/all_to_all | solution.py:208
  389.7 58.0 %all-to-all-start.2 = ((bf16[4,16,16,1152]{3,2,1,0:T(8,128)(2,1)}), bf16[4,16,16,1152]{3,2,1,0:T(8,128)(2,1)}, u32[]{:S(2)}, u32[]{:S(2)}) async-start(bf16[4,16,16,1152]{3,2,1,0:T(8,128)(2,1)} %bitcast.33), calls=%async_computation.2 | async-start | bytes 4718592 | tf_op jit(solution)/shard_map/all_to_all | solution.py:211
  394.2 119.4 %all-gather.14.cloned.1.call-start = ((), (), s32[]{:S(2)}) async-start(), calls=%async_computation.6 | async-start | bytes 11796480 | tf_op jit(solution)/shard_map/all_gather | solution.py:246
  504.9 14.1 %copy-start = (bf16[16,4,4,16,256]{4,3,2,1,0:T(8,128)(2,1)S(1)}, bf16[16,4,4,16,256]{4,3,2,1,0:T(8,128)(2,1)}, u32[]{:S(2)}) copy-start(bf16[16,4,4,16,256]{4,3,2,1,0:T(8,128)(2,1)} %copy.51) | copy-start | bytes 6291460
Sparse Core Ops, SparseCore 0:
  10.1 49.1 all-gather.15
  60.9 171.7 all-gather.9
  234.2 81.6 all-gather.11
  451.2 62.3 all-gather.13

commit v3 on v2

--- a/solution.py
+++ b/solution.py
@@ -4,6 +4,7 @@
 from jax.sharding import PartitionSpec as P
 
 MOST = 16
+PARTS = 2
 
 
 def relocate(gate_up, down, inverse):
@@ -144,6 +145,34 @@
     )
 
 
+def swap_pieces(rows, count, index):
+    shape = rows.shape
+    rows = rows.reshape(*shape[:-1], count // 2, 2, shape[-1] // count)
+    rows = jnp.where(index % 2 == 1, rows[..., ::-1, :], rows)
+    rows = jnp.where(index // 2 == 1, rows[..., ::-1, :, :], rows)
+    return rows.reshape(shape)
+
+
+def spread_weights(weight, part, half):
+    group = lax.axis_index("groups")
+    across = [(i, i ^ 1) for i in range(lax.axis_size("dp"))]
+    beside = [(i, i ^ 2) for i in range(lax.axis_size("dp"))]
+    weight = weight[2 * half * part : 2 * half * (part + 1)]
+    pair = weight.reshape(2, half, *weight.shape[1:])
+    own = jnp.where(group == 1, pair[::-1], pair)
+    first = lax.ppermute(own[0], "dp", beside)
+    own = own.reshape(weight.shape)
+    core = lax.ppermute(own, "dp", across)
+    second = lax.ppermute(first, "groups", [(0, 1), (1, 0)])
+    chip = jnp.concatenate([first, second], axis=0)
+    far = lax.ppermute(chip, "dp", across)
+    return own, core, chip, far
+
+
+def piece_columns(rows, index, share):
+    return rows[..., index * share : (index + 1) * share]
+
+
 def shared_shards(tokens, expert_ids, gate_values, w_gate_up, w_down, new_slot, cotangent):
     expert_peers = lax.axis_size("expert")
     dp_peers = lax.axis_size("dp")
@@ -153,14 +182,22 @@
     hidden_width = w_down.shape[1]
     token_count = tokens.shape[0]
     share = model_width // dp_peers
-    here = me * home_slots + jnp.arange(home_slots, dtype=jnp.int32)
-
-    both = jnp.concatenate([tokens, cotangent], axis=1)
+    dp_index = lax.axis_index("dp")
+    half = home_slots // (2 * PARTS)
+    shift = lax.axis_index("groups") * half
+    here = (me * home_slots + jnp.arange(home_slots, dtype=jnp.int32)) ^ shift
+
+    both = jnp.concatenate(
+        [swap_pieces(tokens, dp_peers, dp_index), swap_pieces(cotangent, dp_peers, dp_index)],
+        axis=1,
+    )
     rows_all = lax.all_gather(both, "expert", axis=0, tiled=False)
     ids_all = lax.all_gather(expert_ids, "expert", axis=0, tiled=False)
     gates_all = lax.all_gather(gate_values, "expert", axis=0, tiled=False)
-    full_gu = lax.all_gather(w_gate_up, "dp", axis=1, tiled=True)
-    full_dn = lax.all_gather(w_down, "dp", axis=2, tiled=True)
+    pieces = [
+        (spread_weights(w_gate_up, part, half), spread_weights(w_down, part, half))
+        for part in range(PARTS)
+    ]
 
     select, cell_gate = cell_select(ids_all, gates_all, here)
     cell_rows = pick_rows("shmt,std->hsmd", select, rows_all)
@@ -172,7 +209,9 @@
     d_outputs = d_outputs.reshape(home_slots, cell_count, model_width)
 
     inverse = jnp.argsort(new_slot).astype(jnp.int32)
-    wide = rows_all.reshape(expert_peers, token_count, 2, dp_peers, share)
+    wide = rows_all.reshape(expert_peers, token_count, 2, model_width)
+    wide = swap_pieces(wide, dp_peers, dp_index)
+    wide = wide.reshape(expert_peers, token_count, 2, dp_peers, share)
     wide = jnp.transpose(wide, (3, 0, 1, 2, 4))
     narrow = lax.all_to_all(wide, "dp", split_axis=0, concat_axis=0, tiled=True)
     narrow = narrow.reshape(dp_peers, expert_peers, token_count, 2 * share)
@@ -191,35 +230,82 @@
         (arrived, d_outputs, new_tokens, new_douts)
     )
 
-    gate_up = jnp.einsum("hrd,hdf->hrf", arrived, full_gu, preferred_element_type=jnp.float32)
-    d_act = jnp.einsum("hrd,hfd->hrf", d_outputs, full_dn, preferred_element_type=jnp.float32)
-    gate_part = gate_up[..., :hidden_width]
-    up_part = gate_up[..., hidden_width:]
-    sigmoid_g = jax.nn.sigmoid(gate_part)
-    silu_g = gate_part * sigmoid_g
-    activation = (silu_g * up_part).astype(jnp.bfloat16)
-    d_gate = d_act * up_part * sigmoid_g * (1.0 + gate_part * (1.0 - sigmoid_g))
-    d_up = d_act * silu_g
-    payload = jnp.concatenate(
-        [d_gate.astype(jnp.bfloat16), d_up.astype(jnp.bfloat16), activation], axis=-1
-    )
+    payloads = []
+    for part, (gu_pieces, dn_pieces) in enumerate(pieces):
+        span = slice(2 * half * part, 2 * half * (part + 1))
+        gate_up = sum(
+            jnp.einsum(
+                "hrd,hdf->hrf",
+                piece_columns(arrived[span], index, share),
+                gu_pieces[index],
+                preferred_element_type=jnp.float32,
+            )
+            for index in range(dp_peers)
+        )
+        d_act = sum(
+            jnp.einsum(
+                "hrd,hfd->hrf",
+                piece_columns(d_outputs[span], index, share),
+                dn_pieces[index],
+                preferred_element_type=jnp.float32,
+            )
+            for index in range(dp_peers)
+        )
+        gate_part = gate_up[..., :hidden_width]
+        up_part = gate_up[..., hidden_width:]
+        sigmoid_g = jax.nn.sigmoid(gate_part)
+        silu_g = gate_part * sigmoid_g
+        activation = (silu_g * up_part).astype(jnp.bfloat16)
+        d_gate = d_act * up_part * sigmoid_g * (1.0 + gate_part * (1.0 - sigmoid_g))
+        d_up = d_act * silu_g
+        payloads.append(
+            jnp.concatenate(
+                [d_gate.astype(jnp.bfloat16), d_up.astype(jnp.bfloat16), activation], axis=-1
+            )
+        )
+    payload = jnp.concatenate(payloads, axis=0)
     pay_shape = (home_slots, expert_peers, MOST, 3 * hidden_width)
     spread = jnp.transpose(payload.reshape(pay_shape), (1, 0, 2, 3))
     spread = lax.all_to_all(spread, "expert", split_axis=0, concat_axis=0, tiled=True)
     spread = spread.reshape(expert_peers * home_slots, MOST, 3 * hidden_width)
-    spread = spread[inverse.reshape(expert_peers, home_slots)]
+    spread = spread[(inverse ^ shift).reshape(expert_peers, home_slots)]
     spread = lax.all_to_all(spread, "expert", split_axis=0, concat_axis=0, tiled=True)
     mine_rows = jnp.transpose(spread, (1, 0, 2, 3)).reshape(
         home_slots, cell_count, 3 * hidden_width
     )
 
-    d_gate_up = payload[..., : 2 * hidden_width]
-    expert_out = jnp.einsum(
-        "hrf,hfd->hrd", activation, full_dn, preferred_element_type=jnp.float32
-    ).astype(jnp.bfloat16)
-    d_rows = jnp.einsum(
-        "hrf,hdf->hrd", d_gate_up, full_gu, preferred_element_type=jnp.float32
-    ).astype(jnp.bfloat16)
+    outs, row_grads = [], []
+    for part_payload, (gu_pieces, dn_pieces) in zip(payloads, pieces):
+        outs.append(
+            jnp.concatenate(
+                [
+                    jnp.einsum(
+                        "hrf,hfd->hrd",
+                        part_payload[..., 2 * hidden_width :],
+                        piece,
+                        preferred_element_type=jnp.float32,
+                    ).astype(jnp.bfloat16)
+                    for piece in dn_pieces
+                ],
+                axis=-1,
+            )
+        )
+        row_grads.append(
+            jnp.concatenate(
+                [
+                    jnp.einsum(
+                        "hrf,hdf->hrd",
+                        part_payload[..., : 2 * hidden_width],
+                        piece,
+                        preferred_element_type=jnp.float32,
+                    ).astype(jnp.bfloat16)
+                    for piece in gu_pieces
+                ],
+                axis=-1,
+            )
+        )
+    expert_out = jnp.concatenate(outs, axis=0)
+    d_rows = jnp.concatenate(row_grads, axis=0)
     cells = (home_slots, expert_peers, MOST, model_width)
     scaled_out = cell_gate[..., None] * expert_out.reshape(cells).astype(jnp.float32)
     part_out = jnp.einsum(
@@ -240,8 +326,8 @@
         tiled=True,
     )
     summed = jnp.sum(back.astype(jnp.float32), axis=0).astype(jnp.bfloat16)
-    layer_out = summed[:, :model_width]
-    d_tokens = summed[:, model_width:]
+    layer_out = swap_pieces(summed[:, :model_width], dp_peers, dp_index)
+    d_tokens = swap_pieces(summed[:, model_width:], dp_peers, dp_index)
 
     group_payload = lax.all_gather(mine_rows, "dp", axis=1, tiled=True)
     grad_gu = jnp.einsum(
@@ -259,10 +345,13 @@
     return (layer_out, d_tokens, grad_gu, grad_dn)
 
 
-def shards(tokens, expert_ids, *rest):
-    if lax.axis_size("expert") < expert_ids.shape[1]:
-        return shared_shards(tokens, expert_ids, *rest)
-    return routed_shards(tokens, expert_ids, *rest)
+def shards(tokens, expert_ids, gate_values, w_gate_up, *rest):
+    few_owners = lax.axis_size("expert") < expert_ids.shape[1]
+    pairs = lax.axis_size("groups") == 2 and lax.axis_size("dp") == 4
+    half = w_gate_up.shape[0] // (2 * PARTS)
+    even = w_gate_up.shape[0] == 2 * PARTS * half and half > 0 and half & (half - 1) == 0
+    body = shared_shards if few_owners and pairs and even else routed_shards
+    return body(tokens, expert_ids, gate_values, w_gate_up, *rest)
 
 
 def solution(mesh):

time: 534 us -> 503 us (0.942); the launches traced: 533 us -> 494 us
  waiting for transfers between devices: 314 us -> 110 us
  local copies, waits for them, and re-layouts: 25.3 us -> 103 us
  blocking collectives: 89.6 us -> 129 us
  matrix products: 67.6 us -> 84.6 us
  other arithmetic: 9.14 us -> 25.6 us
  starting transfers between devices: 13 us -> 26.9 us
    all_gather x2 -> x0, waiting for transfers between devices: 176 us -> none  [the longest x1 109 us: shared_shards(): full_gu = lax.all_gather(w_gate_up, 'dp', axis=1, tiled=True)]
    ppermute x0 -> x16, waiting for transfers between devices: none -> 41.1 us  [the longest x4 41.1 us: spread_weights(): second = lax.ppermute(first, 'groups', [(0, 1), (1, 0)])]
    all_gather x1, blocking collectives: 5.23 us -> 45.5 us  [shared_shards(): ids_group = lax.all_gather(ids_all, 'dp', axis=0, tiled=False)]
    all_to_all x1, waiting for transfers between devices: 35.9 us -> 0.01 us  [shared_shards(): narrow = lax.all_to_all(wide, 'dp', split_axis=0, concat_axis=0, tiled=True)]
    rev x0 -> x5, local copies, waits for them, and re-layouts: none -> 27.2 us  [swap_pieces(): rows = jnp.where(index % 2 == 1, rows[..., ::-1, :], rows)]
    dot_general x4 -> x32, matrix products: 45.7 us -> 65.3 us  [the longest x8 19.8 us: shared_shards(): jnp.einsum('hrf,hdf->hrd', part_payload[..., :2 * hidden_width], piece, p...]
    all_to_all x2, waiting for transfers between devices: 84.6 us -> 65.4 us  [shared_shards(): lax.all_to_all(spread, 'expert', split_axis=0, concat_axis=0, tiled=True)]
    unnamed x14 -> x94, local copies, waits for them, and re-layouts: 0.82 us -> 17.9 us
  transfers between devices with their start and end apart: 7 -> 21, of which waited for: 7 -> 5; matrix products, arithmetic and copies ran while one was open for 13% -> 34% of each run, Pallas kernels for 0% -> 0%
where the time goes in v3:
time: 503 us; the launch traced here: 494 us
  blocking collectives  129 us (26%)
  waiting for transfers between devices  110 us (22%)
  local copies, waits for them, and re-layouts  103 us (20%)
  matrix products  84.6 us (17%)
  starting transfers between devices  26.9 us (5%)
  other arithmetic  25.6 us (5%)
  between operations  15 us (3%)
    all_to_all x2, waiting for transfers between devices, shared_shards(): lax.all_to_all(spread, 'expert', split_axis=0, concat_axis=0, tiled=True)  65.4 us
    all_to_all x1, blocking collectives, shared_shards(): lax.all_to_all(sent, 'expert', split_axis=0, concat_axis=0, tiled=True)  51.1 us
    all_gather x1, blocking collectives, shared_shards(): ids_group = lax.all_gather(ids_all, 'dp', axis=0, tiled=False)  45.5 us
    ppermute x4, waiting for transfers between devices, spread_weights(): second = lax.ppermute(first, 'groups', [(0, 1), (1, 0)])  41.1 us
    rev x5, local copies, waits for them, and re-layouts, swap_pieces(): rows = jnp.where(index % 2 == 1, rows[..., ::-1, :], rows)  27.2 us
    dot_general x8, matrix products, shared_shards(): jnp.einsum('hrf,hdf->hrd', part_payload[..., :2 * hidden_width], piece, p...  19.8 us
    unnamed x94, local copies, waits for them, and re-layouts  17.9 us
    dot_general x8, matrix products, shared_shards(): jnp.einsum('hrf,hfd->hrd', part_payload[..., 2 * hidden_width:], piece, p...  17 us
  transfers between devices with their start and end apart: 21, of which 5 were waited for; matrix products, arithmetic and copies ran while one was open for 34% of the time, Pallas kernels for 0%

profile of v3, /device:TPU:0, one launch (start us, length us, event | category | flops | bytes accessed | tf_op | source)
XLA Modules:
  0.0 494.4 jit_solution(9275467822305428676)
XLA Ops:
  7.2 6.1 %fusion.61 = (bf16[8,256,768]{2,1,0:T(8,128)(2,1)}, bf16[8,256,768]{2,1,0:T(8,128)(2,1)}) fusion(bf16[16,256,768]{2,1,0:T(8,128)(2,1)} %param.10), kind=kLoop, calls=%fused_computation.142 | loop fusion | bytes 12582912 | tf_op jit(solution)/shard_map/slice | solution.py:160
  13.3 3.6 reverse_select_fusion
  18.2 2.9 collective-permute-start.9
  49.5 13.8 %all-gather = s32[512,8]{0,1:T(8,128)S(1)} all-gather(s32[128,8]{0,1:T(8,128)S(1)} %copy-done.42), channel_id=2, replica_groups=mesh['groups'=2,'expert'=4,'dp'=4] {'expert'}, dimensions={0}, use_global_device_ids=true | all-gather | bytes 20480 | tf_op jit(solution)/shard_map/all_gather | solution.py:195
  65.4 13.4 %all-gather.1 = f32[512,8]{0,1:T(8,128)S(1)} all-gather(f32[128,8]{0,1:T(8,128)S(1)} %copy-done.43), channel_id=3, replica_groups=mesh['groups'=2,'expert'=4,'dp'=4] {'expert'}, dimensions={0}, use_global_device_ids=true | all-gather | bytes 20480 | tf_op jit(solution)/shard_map/all_gather | solution.py:196
  78.8 45.5 %all-gather.3 = s32[16,128,8]{1,2,0:T(8,128)S(1)} all-gather(s32[4,128,8]{1,2,0:T(8,128)S(1)} %bitcast.158), channel_id=5, replica_groups=mesh['groups'=2,'expert'=4,'dp'=4] {'dp'}, dimensions={0}, use_global_device_ids=true | all-gather | bytes 81920 | tf_op jit(solution)/shard_map/all_gather | solution.py:218
  124.3 5.4 %all-gather.4 = f32[16,128,8]{1,2,0:T(8,128)S(1)} all-gather(f32[4,128,8]{1,2,0:T(8,128)S(1)} %bitcast.162), channel_id=6, replica_groups=mesh['groups'=2,'expert'=4,'dp'=4] {'dp'}, dimensions={0}, use_global_device_ids=true | all-gather | bytes 81920 | tf_op jit(solution)/shard_map/all_gather | solution.py:219
  138.0 13.2 %collective-permute-done.14 = bf16[4,384,256]{2,1,0:T(8,128)(2,1)S(1)} collective-permute-done((bf16[4,384,256]{2,1,0:T(8,128)(2,1)}, bf16[4,384,256]{2,1,0:T(8,128)(2,1)S(1)}, u32[]{:S(2)}, u32[]{:S(2)}) %collective-permute-start.14) | collective-permute-done | bytes 786464 | tf_op jit(solution)/shard_map/ppermute | solution.py:166
  154.2 4.5 reshape_reshape.6
  158.6 19.3 %rev.46 = bf16[4,128,2,2,2,256]{5,4,3,2,1,0:T(2,128)(2,1)} reverse(bf16[4,128,2,2,2,256]{5,4,3,2,1,0:T(2,128)(2,1)} %reshape_reshape.6), dimensions={4} | reverse | bytes 4194304 | tf_op jit(solution)/shard_map/rev | solution.py:151
  177.9 3.8 broadcast_select_fusion
  183.8 3.1 copy.50
  186.9 4.5 all-to-all-start
  196.6 2.8 constant_dynamic-update-slice_fusion.1
  207.1 27.9 %collective-permute-done.2 = bf16[4,256,768]{2,1,0:T(8,128)(2,1)} collective-permute-done((bf16[4,256,768]{2,1,0:T(8,128)(2,1)}, bf16[4,256,768]{2,1,0:T(8,128)(2,1)}, u32[]{:S(2)}, u32[]{:S(2)}) %collective-permute-start.2) | collective-permute-done | bytes 1572896 | tf_op jit(solution)/shard_map/ppermute | solution.py:166
  237.7 4.4 reshape.178
  242.1 2.9 convolution_bitcast_fusion.1
  286.5 5.1 %all-to-all-start.1 = ((bf16[4,16,16,1152]{3,2,1,0:T(8,128)(2,1)}), bf16[4,16,16,1152]{3,2,1,0:T(8,128)(2,1)}, u32[]{:S(2)}, u32[]{:S(2)}) async-start(bf16[4,16,16,1152]{3,2,1,0:T(8,128)(2,1)} %bitcast.128), calls=%async_computation.1 | async-start | bytes 4718592 | tf_op jit(solution)/shard_map/all_to_all | solution.py:269
  308.4 3.7 convolution_convert_fusion.1
  313.8 32.3 %all-to-all-done.1 = bf16[4,16,16,1152]{3,2,1,0:T(8,128)(2,1)} async-done(((bf16[4,16,16,1152]{3,2,1,0:T(8,128)(2,1)}), bf16[4,16,16,1152]{3,2,1,0:T(8,128)(2,1)}, u32[]{:S(2)}, u32[]{:S(2)}) %all-to-all-start.1) | async-done | bytes 2359328 | tf_op jit(solution)/shard_map/all_to_all | solution.py:269
  346.1 3.9 gather_fusion
  350.0 4.6 all-to-all-start.2
  355.8 3.0 convolution_convert_fusion.5
  358.8 3.1 convolution_convert_fusion.7
  363.0 3.1 convolution_convert_fusion.2
  367.2 3.0 convolution_convert_fusion.6
  375.2 33.1 %all-to-all-done.2 = bf16[4,16,16,1152]{3,2,1,0:T(8,128)(2,1)} async-done(((bf16[4,16,16,1152]{3,2,1,0:T(8,128)(2,1)}), bf16[4,16,16,1152]{3,2,1,0:T(8,128)(2,1)}, u32[]{:S(2)}, u32[]{:S(2)}) %all-to-all-start.2) | async-done | bytes 2359328 | tf_op jit(solution)/shard_map/all_to_all | solution.py:272
  408.3 3.3 copy.56
  411.7 51.1 %all_to_all.20 = bf16[4,128,2048]{2,1,0:T(8,128)(2,1)} all-to-all(bf16[4,128,2048]{2,1,0:T(8,128)(2,1)S(1)} %pad_maximum_fusion), channel_id=1, replica_groups=mesh['groups'=2,'expert'=4,'dp'=4] {'expert'}, dimensions={0} | all-to-all | bytes 4194304 | tf_op jit(solution)/shard_map/all_to_all | solution.py:321
  471.7 3.5 all-gather.8.cloned.1.call-done
  475.2 7.5 %fusion.5 = bf16[16,256,768]{2,1,0:T(8,128)(2,1)} fusion(bf16[16,256,256]{2,1,0:T(8,128)(2,1)S(1)} %bitcast.130, bf16[16,256,1152]{2,1,0:T(8,128)(2,1)} %all-gather.8.cloned.1.call-done), kind=kOutput, calls=%fused_computation.16 | convolution fusion | flops 1613758464 | bytes 14680064 | tf_op jit(solution)/shard_map/hrc,hrf->hcf/dot_general | solution.py:333
  482.7 4.7 fusion.10
  (223 shorter events, 137.3 us)
Async XLA Ops:
  7.2 147.0 %all-gather.10.cloned.1.call-start = ((), (), s32[]{:S(2)}) async-start(), calls=%async_computation.5 | async-start | bytes 2621440 | tf_op jit(solution)/shard_map/all_gather | solution.py:194
  18.2 119.5 %collective-permute-start.9 = (bf16[4,256,768]{2,1,0:T(8,128)(2,1)}, bf16[4,256,768]{2,1,0:T(8,128)(2,1)}, u32[]{:S(2)}, u32[]{:S(2)}) collective-permute-start(bf16[4,256,768]{2,1,0:T(8,128)(2,1)} %slice_bitcast_fusion), channel_id=1, source_target_pairs={{0,2},{1,3},{2,0},{3,1},{4,6},{5,7},{6,4},{7,5},{8,10},{9,11},{10,... | collective-permute-start | bytes 4718600 | tf_op jit(solution)/shard_map/ppermute | solution.py:163
  32.5 232.5 %collective-permute-start.8 = (bf16[8,256,768]{2,1,0:T(8,128)(2,1)S(1)}, bf16[8,256,768]{2,1,0:T(8,128)(2,1)}, u32[]{:S(2)}, u32[]{:S(2)}) collective-permute-start(bf16[8,256,768]{2,1,0:T(8,128)(2,1)S(1)} %bitcast.119), channel_id=1, source_target_pairs={{0,1},{1,0},{2,3},{3,2},{4,5},{5,4},{6,7},{7,6},{8,9},{9,8},{10,11... | collective-permute-start | bytes 9437192 | tf_op jit(solution)/shard_map/ppermute | solution.py:165
  39.9 90.7 %collective-permute-start.13 = (bf16[4,384,256]{2,1,0:T(8,128)(2,1)}, bf16[4,384,256]{2,1,0:T(8,128)(2,1)}, u32[]{:S(2)}, u32[]{:S(2)}) collective-permute-start(bf16[4,384,256]{2,1,0:T(8,128)(2,1)} %slice_bitcast_fusion.2), channel_id=1, source_target_pairs={{0,2},{1,3},{2,0},{3,1},{4,6},{5,7},{6,4},{7,5},{8,10},{9,11},{10,... | collective-permute-start | bytes 2359304 | tf_op jit(solution)/shard_map/ppermute | solution.py:163
  45.1 107.9 %collective-permute-start.1 = (bf16[4,256,768]{2,1,0:T(8,128)(2,1)}, bf16[4,256,768]{2,1,0:T(8,128)(2,1)}, u32[]{:S(2)}, u32[]{:S(2)}) collective-permute-start(bf16[4,256,768]{2,1,0:T(8,128)(2,1)} %slice_bitcast_fusion.1), channel_id=1, source_target_pairs={{0,2},{1,3},{2,0},{3,1},{4,6},{5,7},{6,4},{7,5},{8,10},{9,11},{10,... | collective-permute-start | bytes 4718600 | tf_op jit(solution)/shard_map/ppermute | solution.py:163
  46.8 16.4 %copy-start.44 = (s32[64]{0:T(128)S(1)}, s32[64]{0:T(128)}, u32[]{:S(2)}) copy-start(s32[64]{0:T(128)} %param.12) | copy-start | bytes 772
  46.8 18.6 %copy-start.43 = (f32[128,8]{0,1:T(8,128)S(1)}, f32[128,8]{0,1:T(8,128)}, u32[]{:S(2)}) copy-start(f32[128,8]{0,1:T(8,128)} %param.9) | copy-start | bytes 12292
  49.2 86.3 %collective-permute-start.5 = (bf16[4,384,256]{2,1,0:T(8,128)(2,1)}, bf16[4,384,256]{2,1,0:T(8,128)(2,1)}, u32[]{:S(2)}, u32[]{:S(2)}) collective-permute-start(bf16[4,384,256]{2,1,0:T(8,128)(2,1)} %slice_bitcast_fusion.3), channel_id=1, source_target_pairs={{0,2},{1,3},{2,0},{3,1},{4,6},{5,7},{6,4},{7,5},{8,10},{9,11},{10,... | collective-permute-start | bytes 2359304 | tf_op jit(solution)/shard_map/ppermute | solution.py:163
  130.2 69.2 %copy-start.38 = (s32[4,16,128]{2,1,0:T(8,128)}, s32[4,16,128]{2,1,0:T(8,128)S(1)}, u32[]{:S(2)}) copy-start(s32[4,16,128]{2,1,0:T(8,128)S(1)} %fusion.22) | copy-start | bytes 98308
  130.5 20.6 %collective-permute-start.14 = (bf16[4,384,256]{2,1,0:T(8,128)(2,1)}, bf16[4,384,256]{2,1,0:T(8,128)(2,1)S(1)}, u32[]{:S(2)}, u32[]{:S(2)}) collective-permute-start(bf16[4,384,256]{2,1,0:T(8,128)(2,1)} %collective-permute-done.13), channel_id=1, source_target_pairs={{0,16},{16,0},{1,17},{17,1},{2,18},{18,2},{3,19},{19,3},{4,20},{20... | collective-permute-start | bytes 2359304 | tf_op jit(solution)/shard_map/ppermute | solution.py:166
  132.6 69.9 %copy-start.40 = (f32[4,16,16]{2,1,0:T(8,128)}, f32[4,16,16]{2,1,0:T(8,128)S(1)}, u32[]{:S(2)}) copy-start(f32[4,16,16]{2,1,0:T(8,128)S(1)} %select_reduce_fusion.1) | copy-start | bytes 12292
  135.5 109.5 %collective-permute-start.12 = (bf16[8,384,256]{2,1,0:T(8,128)(2,1)}, bf16[8,384,256]{2,1,0:T(8,128)(2,1)}, u32[]{:S(2)}, u32[]{:S(2)}) collective-permute-start(bf16[8,384,256]{2,1,0:T(8,128)(2,1)} %bitcast.35), channel_id=1, source_target_pairs={{0,1},{1,0},{2,3},{3,2},{4,5},{5,4},{6,7},{7,6},{8,9},{9,8},{10,11... | collective-permute-start | bytes 4718600 | tf_op jit(solution)/shard_map/ppermute | solution.py:165
  137.7 53.8 %collective-permute-start.6 = (bf16[4,384,256]{2,1,0:T(8,128)(2,1)}, bf16[4,384,256]{2,1,0:T(8,128)(2,1)}, u32[]{:S(2)}, u32[]{:S(2)}) collective-permute-start(bf16[4,384,256]{2,1,0:T(8,128)(2,1)} %collective-permute-done.5), channel_id=1, source_target_pairs={{0,16},{16,0},{1,17},{17,1},{2,18},{18,2},{3,19},{19,3},{4,20},{20... | collective-permute-start | bytes 2359304 | tf_op jit(solution)/shard_map/ppermute | solution.py:166
  151.2 53.1 %collective-permute-start.10 = (bf16[4,256,768]{2,1,0:T(8,128)(2,1)}, bf16[4,256,768]{2,1,0:T(8,128)(2,1)}, u32[]{:S(2)}, u32[]{:S(2)}) collective-permute-start(bf16[4,256,768]{2,1,0:T(8,128)(2,1)} %collective-permute-done.9), channel_id=1, source_target_pairs={{0,16},{16,0},{1,17},{17,1},{2,18},{18,2},{3,19},{19,3},{4,20},{20... | collective-permute-start | bytes 4718600 | tf_op jit(solution)/shard_map/ppermute | solution.py:166
  152.9 82.0 %collective-permute-start.2 = (bf16[4,256,768]{2,1,0:T(8,128)(2,1)}, bf16[4,256,768]{2,1,0:T(8,128)(2,1)}, u32[]{:S(2)}, u32[]{:S(2)}) collective-permute-start(bf16[4,256,768]{2,1,0:T(8,128)(2,1)} %collective-permute-done.1), channel_id=1, source_target_pairs={{0,16},{16,0},{1,17},{17,1},{2,18},{18,2},{3,19},{19,3},{4,20},{20... | collective-permute-start | bytes 4718600 | tf_op jit(solution)/shard_map/ppermute | solution.py:166
  186.9 50.7 %all-to-all-start = ((bf16[4,4,128,2,256]{4,3,2,1,0:T(2,128)(2,1)}), bf16[4,4,128,2,256]{4,3,2,1,0:T(2,128)(2,1)}, u32[]{:S(2)}, u32[]{:S(2)}) async-start(bf16[4,4,128,2,256]{4,3,2,1,0:T(2,128)(2,1)} %bitcast.139), calls=%async_computation | async-start | bytes 4194304 | tf_op jit(solution)/shard_map/all_to_all | solution.py:216
  191.4 58.8 %collective-permute-start.15 = (bf16[8,384,256]{2,1,0:T(8,128)(2,1)}, bf16[8,384,256]{2,1,0:T(8,128)(2,1)}, u32[]{:S(2)}, u32[]{:S(2)}) collective-permute-start(bf16[8,384,256]{2,1,0:T(8,128)(2,1)} %constant_dynamic-update-slice_fusion.6), channel_id=1, source_target_pairs={{0,1},{1,0},{2,3},{3,2},{4,5},{5,4},{6,7},{7,6},{8,9},{9,8},{10,11... | collective-permute-start | bytes 4718600 | tf_op jit(solution)/shard_map/ppermute | solution.py:168
  204.3 63.2 %collective-permute-start = (bf16[8,256,768]{2,1,0:T(8,128)(2,1)}, bf16[8,256,768]{2,1,0:T(8,128)(2,1)}, u32[]{:S(2)}, u32[]{:S(2)}) collective-permute-start(bf16[8,256,768]{2,1,0:T(8,128)(2,1)} %bitcast.26), channel_id=1, source_target_pairs={{0,1},{1,0},{2,3},{3,2},{4,5},{5,4},{6,7},{7,6},{8,9},{9,8},{10,11... | collective-permute-start | bytes 9437192 | tf_op jit(solution)/shard_map/ppermute | solution.py:165
  235.0 22.5 %collective-permute-start.7 = (bf16[8,384,256]{2,1,0:T(8,128)(2,1)}, bf16[8,384,256]{2,1,0:T(8,128)(2,1)}, u32[]{:S(2)}, u32[]{:S(2)}) collective-permute-start(bf16[8,384,256]{2,1,0:T(8,128)(2,1)} %constant_dynamic-update-slice_fusion.2), channel_id=1, source_target_pairs={{0,1},{1,0},{2,3},{3,2},{4,5},{5,4},{6,7},{7,6},{8,9},{9,8},{10,11... | collective-permute-start | bytes 4718600 | tf_op jit(solution)/shard_map/ppermute | solution.py:168
  245.0 14.6 %collective-permute-start.4 = (bf16[8,384,256]{2,1,0:T(8,128)(2,1)S(1)}, bf16[8,384,256]{2,1,0:T(8,128)(2,1)S(1)}, u32[]{:S(2)}, u32[]{:S(2)}) collective-permute-start(bf16[8,384,256]{2,1,0:T(8,128)(2,1)S(1)} %bitcast.122), channel_id=1, source_target_pairs={{0,1},{1,0},{2,3},{3,2},{4,5},{5,4},{6,7},{7,6},{8,9},{9,8},{10,11... | collective-permute-start | bytes 4718600 | tf_op jit(solution)/shard_map/ppermute | solution.py:165
  250.2 19.9 %collective-permute-start.11 = (bf16[8,256,768]{2,1,0:T(8,128)(2,1)}, bf16[8,256,768]{2,1,0:T(8,128)(2,1)S(1)}, u32[]{:S(2)}, u32[]{:S(2)}) collective-permute-start(bf16[8,256,768]{2,1,0:T(8,128)(2,1)} %constant_dynamic-update-slice_fusion.4), channel_id=1, source_target_pairs={{0,1},{1,0},{2,3},{3,2},{4,5},{5,4},{6,7},{7,6},{8,9},{9,8},{10,11... | collective-permute-start | bytes 9437192 | tf_op jit(solution)/shard_map/ppermute | solution.py:168
  257.5 19.8 %collective-permute-start.3 = (bf16[8,256,768]{2,1,0:T(8,128)(2,1)}, bf16[8,256,768]{2,1,0:T(8,128)(2,1)S(1)}, u32[]{:S(2)}, u32[]{:S(2)}) collective-permute-start(bf16[8,256,768]{2,1,0:T(8,128)(2,1)} %constant_dynamic-update-slice_fusion), channel_id=1, source_target_pairs={{0,1},{1,0},{2,3},{3,2},{4,5},{5,4},{6,7},{7,6},{8,9},{9,8},{10,11... | collective-permute-start | bytes 9437192 | tf_op jit(solution)/shard_map/ppermute | solution.py:168
  277.3 6.6 %copy-start.8 = (bf16[8,64,384]{2,1,0:T(8,128)(2,1)}, bf16[8,64,384]{2,1,0:T(8,128)(2,1)S(1)}, u32[]{:S(2)}) copy-start(bf16[8,64,384]{2,1,0:T(8,128)(2,1)S(1)} %get-tuple-element.25) | copy-start | bytes 1179652
  277.3 6.6 %copy-start.20 = (bf16[8,64,384]{2,1,0:T(8,128)(2,1)}, bf16[8,64,384]{2,1,0:T(8,128)(2,1)S(1)}, u32[]{:S(2)}) copy-start(bf16[8,64,384]{2,1,0:T(8,128)(2,1)S(1)} %get-tuple-element.27) | copy-start | bytes 1179652
  286.5 59.7 %all-to-all-start.1 = ((bf16[4,16,16,1152]{3,2,1,0:T(8,128)(2,1)}), bf16[4,16,16,1152]{3,2,1,0:T(8,128)(2,1)}, u32[]{:S(2)}, u32[]{:S(2)}) async-start(bf16[4,16,16,1152]{3,2,1,0:T(8,128)(2,1)} %bitcast.128), calls=%async_computation.1 | async-start | bytes 4718592 | tf_op jit(solution)/shard_map/all_to_all | solution.py:269
  291.8 5.4 %copy-start.18 = (bf16[8,64,384]{2,1,0:T(8,128)(2,1)S(1)}, bf16[8,64,384]{2,1,0:T(8,128)(2,1)}, u32[]{:S(2)}) copy-start(bf16[8,64,384]{2,1,0:T(8,128)(2,1)} %copy-done.17) | copy-start | bytes 1179652
  294.5 5.2 %copy-start.2 = (bf16[2,4,384,256]{3,2,1,0:T(8,128)(2,1)S(1)}, bf16[2,4,384,256]{3,2,1,0:T(8,128)(2,1)}, u32[]{:S(2)}) copy-start(bf16[2,4,384,256]{3,2,1,0:T(8,128)(2,1)} %copy-done) | copy-start | bytes 4718596
  350.0 5.1 %copy-start.27 = (bf16[8,384,256]{2,1,0:T(8,128)(2,1)S(1)}, bf16[8,384,256]{2,1,0:T(8,128)(2,1)}, u32[]{:S(2)}) copy-start(bf16[8,384,256]{2,1,0:T(8,128)(2,1)} %copy-done.26) | copy-start | bytes 4718596
  350.0 58.3 %all-to-all-start.2 = ((bf16[4,16,16,1152]{3,2,1,0:T(8,128)(2,1)}), bf16[4,16,16,1152]{3,2,1,0:T(8,128)(2,1)}, u32[]{:S(2)}, u32[]{:S(2)}) async-start(bf16[4,16,16,1152]{3,2,1,0:T(8,128)(2,1)} %bitcast.46), calls=%async_computation.2 | async-start | bytes 4718592 | tf_op jit(solution)/shard_map/all_to_all | solution.py:272
  354.6 120.5 %all-gather.8.cloned.1.call-start = ((), (), s32[]{:S(2)}) async-start(), calls=%async_computation.4 | async-start | bytes 11796480 | tf_op jit(solution)/shard_map/all_gather | solution.py:332
  466.7 8.5 %copy-start.22 = (bf16[16,4,4,16,256]{4,3,2,1,0:T(8,128)(2,1)S(1)}, bf16[16,4,4,16,256]{4,3,2,1,0:T(8,128)(2,1)}, u32[]{:S(2)}) copy-start(bf16[16,4,4,16,256]{4,3,2,1,0:T(8,128)(2,1)} %copy.51) | copy-start | bytes 6291460
  475.2 7.5 %copy-start.24 = (bf16[16,4,4,16,256]{4,3,2,1,0:T(8,128)(2,1)S(1)}, bf16[16,4,4,16,256]{4,3,2,1,0:T(8,128)(2,1)}, u32[]{:S(2)}) copy-start(bf16[16,4,4,16,256]{4,3,2,1,0:T(8,128)(2,1)} %copy.52) | copy-start | bytes 6291460
  (34 other events, 73.2 us)
Sparse Core Ops, SparseCore 0:
  32.6 47.8 all-gather.9
  411.8 63.3 all-gather.7

commit v4 on v3

--- a/solution.py
+++ b/solution.py
@@ -192,8 +192,16 @@
         axis=1,
     )
     rows_all = lax.all_gather(both, "expert", axis=0, tiled=False)
-    ids_all = lax.all_gather(expert_ids, "expert", axis=0, tiled=False)
-    gates_all = lax.all_gather(gate_values, "expert", axis=0, tiled=False)
+    routing = jnp.concatenate([expert_ids.astype(jnp.float32).T, gate_values.T], axis=0)
+    routing = lax.all_gather(routing, ("expert", "dp"), axis=0, tiled=False)
+    routing, w_gate_up, w_down = lax.optimization_barrier((routing, w_gate_up, w_down))
+    routing = routing.reshape(expert_peers, dp_peers, *routing.shape[1:])
+    routing = jnp.transpose(routing, (1, 0, 3, 2))
+    top_count = expert_ids.shape[1]
+    ids_group = routing[..., :top_count].astype(jnp.int32)
+    gates_group = routing[..., top_count:]
+    ids_all = lax.dynamic_index_in_dim(ids_group, dp_index, 0, keepdims=False)
+    gates_all = lax.dynamic_index_in_dim(gates_group, dp_index, 0, keepdims=False)
     pieces = [
         (spread_weights(w_gate_up, part, half), spread_weights(w_down, part, half))
         for part in range(PARTS)
@@ -209,27 +217,7 @@
     d_outputs = d_outputs.reshape(home_slots, cell_count, model_width)
 
     inverse = jnp.argsort(new_slot).astype(jnp.int32)
-    wide = rows_all.reshape(expert_peers, token_count, 2, model_width)
-    wide = swap_pieces(wide, dp_peers, dp_index)
-    wide = wide.reshape(expert_peers, token_count, 2, dp_peers, share)
-    wide = jnp.transpose(wide, (3, 0, 1, 2, 4))
-    narrow = lax.all_to_all(wide, "dp", split_axis=0, concat_axis=0, tiled=True)
-    narrow = narrow.reshape(dp_peers, expert_peers, token_count, 2 * share)
-    ids_group = lax.all_gather(ids_all, "dp", axis=0, tiled=False)
-    gates_group = lax.all_gather(gates_all, "dp", axis=0, tiled=False)
     mine = lax.dynamic_slice_in_dim(inverse, me * home_slots, home_slots)
-    select_new, gate_new = cell_select(ids_group, gates_group, mine)
-    new_rows = pick_rows("pshmt,pstc->hpsmc", select_new, narrow)
-    gate_new = jnp.transpose(gate_new, (2, 0, 1, 3))
-    group_rows = dp_peers * cell_count
-    new_tokens = new_rows[..., :share].astype(jnp.bfloat16)
-    new_tokens = new_tokens.reshape(home_slots, group_rows, share)
-    new_douts = (gate_new[..., None] * new_rows[..., share:]).astype(jnp.bfloat16)
-    new_douts = new_douts.reshape(home_slots, group_rows, share)
-    arrived, d_outputs, new_tokens, new_douts = lax.optimization_barrier(
-        (arrived, d_outputs, new_tokens, new_douts)
-    )
-
     payloads = []
     for part, (gu_pieces, dn_pieces) in enumerate(pieces):
         span = slice(2 * half * part, 2 * half * (part + 1))
@@ -263,10 +251,40 @@
                 [d_gate.astype(jnp.bfloat16), d_up.astype(jnp.bfloat16), activation], axis=-1
             )
         )
-    payload = jnp.concatenate(payloads, axis=0)
-    pay_shape = (home_slots, expert_peers, MOST, 3 * hidden_width)
-    spread = jnp.transpose(payload.reshape(pay_shape), (1, 0, 2, 3))
-    spread = lax.all_to_all(spread, "expert", split_axis=0, concat_axis=0, tiled=True)
+    last = payloads[-1]
+    rows_all, last = lax.optimization_barrier((rows_all, last))
+    payloads[-1] = last
+    wide = rows_all.reshape(expert_peers, token_count, 2, dp_peers, share)
+    narrow = [wide[..., 0, :]]
+    for index in range(1, dp_peers):
+        partners = [(i, i ^ index) for i in range(dp_peers)]
+        narrow.append(lax.ppermute(wide[..., index, :], "dp", partners))
+    narrow = jnp.stack(narrow).reshape(dp_peers // 2, 2, expert_peers, token_count, 2 * share)
+    narrow = jnp.where(dp_index % 2 == 1, narrow[:, ::-1], narrow)
+    narrow = jnp.where(dp_index // 2 == 1, narrow[::-1], narrow)
+    narrow = narrow.reshape(dp_peers, expert_peers, token_count, 2 * share)
+    select_new, gate_new = cell_select(ids_group, gates_group, mine)
+    new_rows = pick_rows("pshmt,pstc->hpsmc", select_new, narrow)
+    gate_new = jnp.transpose(gate_new, (2, 0, 1, 3))
+    group_rows = dp_peers * cell_count
+    new_tokens = new_rows[..., :share].astype(jnp.bfloat16)
+    new_tokens = new_tokens.reshape(home_slots, group_rows, share)
+    new_douts = (gate_new[..., None] * new_rows[..., share:]).astype(jnp.bfloat16)
+    new_douts = new_douts.reshape(home_slots, group_rows, share)
+    pay_shape = (2 * half, expert_peers, MOST, 3 * hidden_width)
+    spread = jnp.concatenate(
+        [
+            lax.all_to_all(
+                jnp.transpose(part_payload.reshape(pay_shape), (1, 0, 2, 3)),
+                "expert",
+                split_axis=0,
+                concat_axis=0,
+                tiled=True,
+            )
+            for part_payload in payloads
+        ],
+        axis=1,
+    )
     spread = spread.reshape(expert_peers * home_slots, MOST, 3 * hidden_width)
     spread = spread[(inverse ^ shift).reshape(expert_peers, home_slots)]
     spread = lax.all_to_all(spread, "expert", split_axis=0, concat_axis=0, tiled=True)

time: 503 us -> 504 us (level)
  waiting for transfers between devices: 110 us -> 243 us
  blocking collectives: 129 us -> 23.4 us
  local copies, waits for them, and re-layouts: 103 us -> 77.4 us
    ppermute x4, waiting for transfers between devices: 0.01 us -> 73.1 us  [spread_weights(): first = lax.ppermute(own[0], 'dp', beside)]
    all_gather x4 -> x1, blocking collectives: 78.1 us -> 23.4 us  [shared_shards(): routing = lax.all_gather(routing, ('expert', 'dp'), axis=0, tiled=False)]
    all_to_all x1 -> x0, blocking collectives: 51.1 us -> none  [shared_shards(): lax.all_to_all(sent, 'expert', split_axis=0, concat_axis=0, tiled=True)]
    ppermute x0 -> x3, waiting for transfers between devices: none -> 43.4 us  [shared_shards(): narrow.append(lax.ppermute(wide[..., index, :], 'dp', partners))]
    all_to_all x2 -> x1, waiting for transfers between devices: 65.4 us -> 33.8 us  [shared_shards(): lax.all_to_all(spread, 'expert', split_axis=0, concat_axis=0, tiled=True)]
    all_to_all x1 -> x3, waiting for transfers between devices: 0.01 us -> 24.6 us  [the longest x2 24.6 us: shared_shards(): lax.all_to_all(jnp.transpose(part_payload.reshape(pay_shape), (1, 0, 2, 3...]
    rev x5 -> x4, local copies, waits for them, and re-layouts: 27.2 us -> 7.47 us  [swap_pieces(): rows = jnp.where(index % 2 == 1, rows[..., ::-1, :], rows)]
    ppermute x4, waiting for transfers between devices: 41.1 us -> 60.3 us  [spread_weights(): second = lax.ppermute(first, 'groups', [(0, 1), (1, 0)])]
  transfers between devices with their start and end apart: 21 -> 25, of which waited for: 5 -> 11; matrix products, arithmetic and copies ran while one was open for 34% -> 28% of each run, Pallas kernels for 0% -> 0%
where the time goes in v4:
time: 504 us; the launch traced here: 499 us
  waiting for transfers between devices  243 us (48%)
  matrix products  81.6 us (16%)
  local copies, waits for them, and re-layouts  77.4 us (15%)
  starting transfers between devices  30.8 us (6%)
  other arithmetic  27.4 us (5%)
  blocking collectives  23.4 us (5%)
  between operations  15.2 us (3%)
    ppermute x4, waiting for transfers between devices, spread_weights(): first = lax.ppermute(own[0], 'dp', beside)  73.1 us
    ppermute x4, waiting for transfers between devices, spread_weights(): second = lax.ppermute(first, 'groups', [(0, 1), (1, 0)])  60.3 us
    ppermute x3, waiting for transfers between devices, shared_shards(): narrow.append(lax.ppermute(wide[..., index, :], 'dp', partners))  43.4 us
    all_to_all x1, waiting for transfers between devices, shared_shards(): lax.all_to_all(spread, 'expert', split_axis=0, concat_axis=0, tiled=True)  33.8 us
    all_to_all x2, waiting for transfers between devices, shared_shards(): lax.all_to_all(jnp.transpose(part_payload.reshape(pay_shape), (1, 0, 2, 3...  24.6 us
    all_gather x1, blocking collectives, shared_shards(): routing = lax.all_gather(routing, ('expert', 'dp'), axis=0, tiled=False)  23.4 us
    unnamed x94, local copies, waits for them, and re-layouts  19.9 us
    dot_general x8, matrix products, shared_shards(): jnp.einsum('hrf,hdf->hrd', part_payload[..., :2 * hidden_width], piece, p...  18.6 us
  transfers between devices with their start and end apart: 25, of which 11 were waited for; matrix products, arithmetic and copies ran while one was open for 28% of the time, Pallas kernels for 0%

profile of v4, /device:TPU:0, one launch (start us, length us, event | category | flops | bytes accessed | tf_op | source)
XLA Modules:
  0.0 498.9 jit_solution(8560787140409708609)
XLA Ops:
  8.6 23.4 %all-gather = f32[256,128]{1,0:T(8,128)S(1)} all-gather(f32[16,128]{1,0:T(8,128)S(1)} %pad_maximum_fusion.7), channel_id=2, replica_groups=mesh['groups'=2,'expert'=4,'dp'=4] {'expert','dp'}, dimensions={0}, use_global_device_ids=true | all-gather | bytes 139264 | tf_op jit(solution)/shard_map/all_gather | solution.py:196
  32.0 6.1 %fusion.68 = (bf16[8,256,768]{2,1,0:T(8,128)(2,1)}, bf16[8,256,768]{2,1,0:T(8,128)(2,1)}) fusion(bf16[16,256,768]{2,1,0:T(8,128)(2,1)} %param.10), kind=kLoop, calls=%fused_computation.160 | loop fusion | bytes 12582912 | tf_op jit(solution)/shard_map/slice | solution.py:160
  38.1 3.6 reverse_select_fusion
  72.6 24.8 %collective-permute-done.9 = bf16[4,384,256]{2,1,0:T(8,128)(2,1)} collective-permute-done((bf16[4,384,256]{2,1,0:T(8,128)(2,1)}, bf16[4,384,256]{2,1,0:T(8,128)(2,1)}, u32[]{:S(2)}, u32[]{:S(2)}) %collective-permute-start.9) | collective-permute-done | bytes 786464 | tf_op jit(solution)/shard_map/ppermute | solution.py:163
  99.2 48.3 %collective-permute-done.5 = bf16[4,384,256]{2,1,0:T(8,128)(2,1)} collective-permute-done((bf16[4,384,256]{2,1,0:T(8,128)(2,1)}, bf16[4,384,256]{2,1,0:T(8,128)(2,1)}, u32[]{:S(2)}, u32[]{:S(2)}) %collective-permute-start.5) | collective-permute-done | bytes 786464 | tf_op jit(solution)/shard_map/ppermute | solution.py:163
  158.9 9.2 %collective-permute-done.6 = bf16[4,384,256]{2,1,0:T(8,128)(2,1)S(1)} collective-permute-done((bf16[4,384,256]{2,1,0:T(8,128)(2,1)}, bf16[4,384,256]{2,1,0:T(8,128)(2,1)S(1)}, u32[]{:S(2)}, u32[]{:S(2)}) %collective-permute-start.6) | collective-permute-done | bytes 786464 | tf_op jit(solution)/shard_map/ppermute | solution.py:166
  173.3 2.8 fusion.75
  178.5 23.4 %collective-permute-done.14 = bf16[4,256,768]{2,1,0:T(8,128)(2,1)} collective-permute-done((bf16[4,256,768]{2,1,0:T(8,128)(2,1)}, bf16[4,256,768]{2,1,0:T(8,128)(2,1)}, u32[]{:S(2)}, u32[]{:S(2)}) %collective-permute-start.14) | collective-permute-done | bytes 1572896 | tf_op jit(solution)/shard_map/ppermute | solution.py:166
  206.5 27.6 %collective-permute-done.2 = bf16[4,256,768]{2,1,0:T(8,128)(2,1)} collective-permute-done((bf16[4,256,768]{2,1,0:T(8,128)(2,1)}, bf16[4,256,768]{2,1,0:T(8,128)(2,1)}, u32[]{:S(2)}, u32[]{:S(2)}) %collective-permute-start.2) | collective-permute-done | bytes 1572896 | tf_op jit(solution)/shard_map/ppermute | solution.py:166
  260.5 4.3 all-to-all-start.1
  267.6 2.9 add_add_fusion.1
  282.9 11.5 %all-to-all-done.1 = bf16[4,8,16,1152]{3,2,1,0:T(8,128)(2,1)} async-done(((bf16[4,8,16,1152]{3,2,1,0:T(8,128)(2,1)}), bf16[4,8,16,1152]{3,2,1,0:T(8,128)(2,1)}, u32[]{:S(2)}, u32[]{:S(2)}) %all-to-all-start.1) | async-done | bytes 1179680 | tf_op jit(solution)/shard_map/all_to_all | solution.py:277
  294.4 3.5 all-to-all-start
  304.2 3.8 convolution_convert_fusion.5
  309.8 3.7 convolution_convert_fusion.4
  313.5 13.1 %all-to-all-done = bf16[4,8,16,1152]{3,2,1,0:T(8,128)(2,1)S(1)} async-done(((bf16[4,8,16,1152]{3,2,1,0:T(8,128)(2,1)}), bf16[4,8,16,1152]{3,2,1,0:T(8,128)(2,1)S(1)}, u32[]{:S(2)}, u32[]{:S(2)}) %all-to-all-start) | async-done | bytes 1179680 | tf_op jit(solution)/shard_map/all_to_all | solution.py:277
  326.6 2.9 pad_maximum_fusion
  329.4 3.9 gather_fusion
  333.4 4.5 all-to-all-start.2
  339.8 3.1 convolution_convert_fusion.6
  347.8 3.0 convolution_convert_fusion.2
  357.5 33.8 %all-to-all-done.2 = bf16[4,16,16,1152]{3,2,1,0:T(8,128)(2,1)} async-done(((bf16[4,16,16,1152]{3,2,1,0:T(8,128)(2,1)}), bf16[4,16,16,1152]{3,2,1,0:T(8,128)(2,1)}, u32[]{:S(2)}, u32[]{:S(2)}) %all-to-all-start.2) | async-done | bytes 2359328 | tf_op jit(solution)/shard_map/all_to_all | solution.py:290
  391.3 3.3 copy.70
  394.7 4.6 all-to-all-start.3
  399.6 3.5 reshape.170
  403.1 3.2 fusion.71
  409.9 22.0 %collective-permute-done.18 = bf16[4,128,2,256]{3,1,2,0:T(8,128)(2,1)S(1)} collective-permute-done((bf16[4,128,2,256]{3,1,2,0:T(8,128)(2,1)S(1)}, bf16[4,128,2,256]{3,1,2,0:T(8,128)(2,1)S(1)}, u32[]{:S(2)}, u32[]{:S(2)}) %collective-permute-start.18) | collective-permute-done | bytes 524320 | tf_op jit(solution)/shard_map/ppermute | solution.py:261
  431.8 21.4 %collective-permute-done.17 = bf16[4,128,2,256]{3,1,2,0:T(8,128)(2,1)S(1)} collective-permute-done((bf16[4,128,2,256]{3,1,2,0:T(8,128)(2,1)S(1)}, bf16[4,128,2,256]{3,1,2,0:T(8,128)(2,1)S(1)}, u32[]{:S(2)}, u32[]{:S(2)}) %collective-permute-start.17) | collective-permute-done | bytes 524320 | tf_op jit(solution)/shard_map/ppermute | solution.py:261
  455.9 2.8 reverse_select_fusion.3
  471.9 7.8 %all-gather.5.cloned.1.call-done = bf16[16,256,1152]{2,1,0:T(8,128)(2,1)} async-done(((bf16[16,64,1152]{2,1,0:T(8,128)(2,1)}), bf16[16,256,1152]{2,1,0:T(8,128)(2,1)}) %all-gather.5.cloned.1.call-update) | async-done | bytes 9437200 | tf_op jit(solution)/shard_map/all_gather | solution.py:350
  479.7 7.5 %fusion.5 = bf16[16,256,768]{2,1,0:T(8,128)(2,1)} fusion(bf16[16,256,256]{2,1,0:T(8,128)(2,1)S(1)} %bitcast.160, bf16[16,256,1152]{2,1,0:T(8,128)(2,1)} %all-gather.5.cloned.1.call-done), kind=kOutput, calls=%fused_computation.13 | convolution fusion | flops 1613758464 | bytes 14680064 | tf_op jit(solution)/shard_map/hrc,hrf->hcf/dot_general | solution.py:351
  487.2 4.7 fusion.10
  (238 shorter events, 139.7 us)
Async XLA Ops:
  7.2 166.1 %all-gather.7.cloned.1.call-start = ((), (), s32[]{:S(2)}) async-start(), calls=%async_computation.5 | async-start | bytes 2621440 | tf_op jit(solution)/shard_map/all_gather | solution.py:194
  41.7 205.4 %copy-start = (bf16[2,4,256,768]{3,2,1,0:T(8,128)(2,1)}, bf16[2,4,256,768]{3,2,1,0:T(8,128)(2,1)S(1)}, u32[]{:S(2)}) copy-start(bf16[2,4,256,768]{3,2,1,0:T(8,128)(2,1)S(1)} %reverse_select_fusion) | copy-start | bytes 9437188
  43.1 110.3 %collective-permute-start.13 = (bf16[4,256,768]{2,1,0:T(8,128)(2,1)}, bf16[4,256,768]{2,1,0:T(8,128)(2,1)}, u32[]{:S(2)}, u32[]{:S(2)}) collective-permute-start(bf16[4,256,768]{2,1,0:T(8,128)(2,1)} %slice_bitcast_fusion), channel_id=1, source_target_pairs={{0,2},{1,3},{2,0},{3,1},{4,6},{5,7},{6,4},{7,5},{8,10},{9,11},{10,... | collective-permute-start | bytes 4718600 | tf_op jit(solution)/shard_map/ppermute | solution.py:163
  54.8 194.7 %collective-permute-start.12 = (bf16[8,256,768]{2,1,0:T(8,128)(2,1)S(1)}, bf16[8,256,768]{2,1,0:T(8,128)(2,1)}, u32[]{:S(2)}, u32[]{:S(2)}) collective-permute-start(bf16[8,256,768]{2,1,0:T(8,128)(2,1)S(1)} %bitcast.145), channel_id=1, source_target_pairs={{0,1},{1,0},{2,3},{3,2},{4,5},{5,4},{6,7},{7,6},{8,9},{9,8},{10,11... | collective-permute-start | bytes 9437192 | tf_op jit(solution)/shard_map/ppermute | solution.py:165
  63.0 34.4 %collective-permute-start.9 = (bf16[4,384,256]{2,1,0:T(8,128)(2,1)}, bf16[4,384,256]{2,1,0:T(8,128)(2,1)}, u32[]{:S(2)}, u32[]{:S(2)}) collective-permute-start(bf16[4,384,256]{2,1,0:T(8,128)(2,1)} %slice_bitcast_fusion.2), channel_id=1, source_target_pairs={{0,2},{1,3},{2,0},{3,1},{4,6},{5,7},{6,4},{7,5},{8,10},{9,11},{10,... | collective-permute-start | bytes 2359304 | tf_op jit(solution)/shard_map/ppermute | solution.py:163
  66.4 92.3 %collective-permute-start.1 = (bf16[4,256,768]{2,1,0:T(8,128)(2,1)}, bf16[4,256,768]{2,1,0:T(8,128)(2,1)}, u32[]{:S(2)}, u32[]{:S(2)}) collective-permute-start(bf16[4,256,768]{2,1,0:T(8,128)(2,1)} %slice_bitcast_fusion.1), channel_id=1, source_target_pairs={{0,2},{1,3},{2,0},{3,1},{4,6},{5,7},{6,4},{7,5},{8,10},{9,11},{10,... | collective-permute-start | bytes 4718600 | tf_op jit(solution)/shard_map/ppermute | solution.py:163
  68.7 78.8 %collective-permute-start.5 = (bf16[4,384,256]{2,1,0:T(8,128)(2,1)}, bf16[4,384,256]{2,1,0:T(8,128)(2,1)}, u32[]{:S(2)}, u32[]{:S(2)}) collective-permute-start(bf16[4,384,256]{2,1,0:T(8,128)(2,1)} %slice_bitcast_fusion.3), channel_id=1, source_target_pairs={{0,2},{1,3},{2,0},{3,1},{4,6},{5,7},{6,4},{7,5},{8,10},{9,11},{10,... | collective-permute-start | bytes 2359304 | tf_op jit(solution)/shard_map/ppermute | solution.py:163
  72.2 83.8 %copy-start.34 = (s32[4,4,128,8]{2,3,0,1:T(8,128)}, s32[4,4,128,8]{2,3,0,1:T(8,128)S(1)}, u32[]{:S(2)}) copy-start(s32[4,4,128,8]{2,3,0,1:T(8,128)S(1)} %get-tuple-element.41) | copy-start | bytes 196612
  72.2 83.8 %copy-start.36 = (f32[4,4,128,8]{2,3,0,1:T(8,128)}, f32[4,4,128,8]{2,3,0,1:T(8,128)S(1)}, u32[]{:S(2)}) copy-start(f32[4,4,128,8]{2,3,0,1:T(8,128)S(1)} %get-tuple-element.40) | copy-start | bytes 196612
  72.6 100.7 %copy-start.38 = (s32[4,16,128]{2,1,0:T(8,128)}, s32[4,16,128]{2,1,0:T(8,128)S(1)}, u32[]{:S(2)}) copy-start(s32[4,16,128]{2,1,0:T(8,128)S(1)} %fusion.21) | copy-start | bytes 98308
  97.5 58.6 %collective-permute-start.10 = (bf16[4,384,256]{2,1,0:T(8,128)(2,1)}, bf16[4,384,256]{2,1,0:T(8,128)(2,1)}, u32[]{:S(2)}, u32[]{:S(2)}) collective-permute-start(bf16[4,384,256]{2,1,0:T(8,128)(2,1)} %collective-permute-done.9), channel_id=1, source_target_pairs={{0,16},{16,0},{1,17},{17,1},{2,18},{18,2},{3,19},{19,3},{4,20},{20... | collective-permute-start | bytes 2359304 | tf_op jit(solution)/shard_map/ppermute | solution.py:166
  147.5 20.7 %collective-permute-start.6 = (bf16[4,384,256]{2,1,0:T(8,128)(2,1)}, bf16[4,384,256]{2,1,0:T(8,128)(2,1)S(1)}, u32[]{:S(2)}, u32[]{:S(2)}) collective-permute-start(bf16[4,384,256]{2,1,0:T(8,128)(2,1)} %collective-permute-done.5), channel_id=1, source_target_pairs={{0,16},{16,0},{1,17},{17,1},{2,18},{18,2},{3,19},{19,3},{4,20},{20... | collective-permute-start | bytes 2359304 | tf_op jit(solution)/shard_map/ppermute | solution.py:166
  153.4 23.3 %collective-permute-start.8 = (bf16[8,384,256]{2,1,0:T(8,128)(2,1)}, bf16[8,384,256]{2,1,0:T(8,128)(2,1)}, u32[]{:S(2)}, u32[]{:S(2)}) collective-permute-start(bf16[8,384,256]{2,1,0:T(8,128)(2,1)} %bitcast.25), channel_id=1, source_target_pairs={{0,1},{1,0},{2,3},{3,2},{4,5},{5,4},{6,7},{7,6},{8,9},{9,8},{10,11... | collective-permute-start | bytes 4718600 | tf_op jit(solution)/shard_map/ppermute | solution.py:165
  156.1 45.9 %collective-permute-start.14 = (bf16[4,256,768]{2,1,0:T(8,128)(2,1)}, bf16[4,256,768]{2,1,0:T(8,128)(2,1)}, u32[]{:S(2)}, u32[]{:S(2)}) collective-permute-start(bf16[4,256,768]{2,1,0:T(8,128)(2,1)} %collective-permute-done.13), channel_id=1, source_target_pairs={{0,16},{16,0},{1,17},{17,1},{2,18},{18,2},{3,19},{19,3},{4,20},{20... | collective-permute-start | bytes 4718600 | tf_op jit(solution)/shard_map/ppermute | solution.py:166
  158.7 78.1 %collective-permute-start.11 = (bf16[8,384,256]{2,1,0:T(8,128)(2,1)}, bf16[8,384,256]{2,1,0:T(8,128)(2,1)}, u32[]{:S(2)}, u32[]{:S(2)}) collective-permute-start(bf16[8,384,256]{2,1,0:T(8,128)(2,1)} %constant_dynamic-update-slice_fusion.4), channel_id=1, source_target_pairs={{0,1},{1,0},{2,3},{3,2},{4,5},{5,4},{6,7},{7,6},{8,9},{9,8},{10,11... | collective-permute-start | bytes 4718600 | tf_op jit(solution)/shard_map/ppermute | solution.py:168
  168.1 66.0 %collective-permute-start.2 = (bf16[4,256,768]{2,1,0:T(8,128)(2,1)}, bf16[4,256,768]{2,1,0:T(8,128)(2,1)}, u32[]{:S(2)}, u32[]{:S(2)}) collective-permute-start(bf16[4,256,768]{2,1,0:T(8,128)(2,1)} %collective-permute-done.1), channel_id=1, source_target_pairs={{0,16},{16,0},{1,17},{17,1},{2,18},{18,2},{3,19},{19,3},{4,20},{20... | collective-permute-start | bytes 4718600 | tf_op jit(solution)/shard_map/ppermute | solution.py:166
  178.5 73.6 %collective-permute-start = (bf16[8,256,768]{2,1,0:T(8,128)(2,1)S(1)}, bf16[8,256,768]{2,1,0:T(8,128)(2,1)S(1)}, u32[]{:S(2)}, u32[]{:S(2)}) collective-permute-start(bf16[8,256,768]{2,1,0:T(8,128)(2,1)S(1)} %bitcast.148), channel_id=1, source_target_pairs={{0,1},{1,0},{2,3},{3,2},{4,5},{5,4},{6,7},{7,6},{8,9},{9,8},{10,11... | collective-permute-start | bytes 9437192 | tf_op jit(solution)/shard_map/ppermute | solution.py:165
  202.0 42.0 %collective-permute-start.4 = (bf16[8,384,256]{2,1,0:T(8,128)(2,1)S(1)}, bf16[8,384,256]{2,1,0:T(8,128)(2,1)S(1)}, u32[]{:S(2)}, u32[]{:S(2)}) collective-permute-start(bf16[8,384,256]{2,1,0:T(8,128)(2,1)S(1)} %bitcast.151), channel_id=1, source_target_pairs={{0,1},{1,0},{2,3},{3,2},{4,5},{5,4},{6,7},{7,6},{8,9},{9,8},{10,11... | collective-permute-start | bytes 4718600 | tf_op jit(solution)/shard_map/ppermute | solution.py:165
  202.5 49.6 %copy-start.20 = (bf16[8,4,16,1024]{3,2,1,0:T(8,128)(2,1)}, bf16[8,4,16,1024]{3,2,1,0:T(8,128)(2,1)S(1)}, u32[]{:S(2)}) copy-start(bf16[8,4,16,1024]{3,2,1,0:T(8,128)(2,1)S(1)} %copy.62) | copy-start | bytes 3145732
  204.6 40.9 %copy-start.21 = (bf16[8,4,16,1024]{3,2,1,0:T(8,128)(2,1)}, bf16[8,4,16,1024]{3,2,1,0:T(8,128)(2,1)S(1)}, u32[]{:S(2)}) copy-start(bf16[8,4,16,1024]{3,2,1,0:T(8,128)(2,1)S(1)} %copy.66) | copy-start | bytes 3145732
  206.5 49.7 %copy-start.6 = (bf16[8,256,768]{2,1,0:T(8,128)(2,1)}, bf16[8,256,768]{2,1,0:T(8,128)(2,1)S(1)}, u32[]{:S(2)}) copy-start(bf16[8,256,768]{2,1,0:T(8,128)(2,1)S(1)} %constant_dynamic-update-slice_fusion.6) | copy-start | bytes 9437188
  234.2 11.4 %collective-permute-start.7 = (bf16[8,384,256]{2,1,0:T(8,128)(2,1)}, bf16[8,384,256]{2,1,0:T(8,128)(2,1)S(1)}, u32[]{:S(2)}, u32[]{:S(2)}) collective-permute-start(bf16[8,384,256]{2,1,0:T(8,128)(2,1)} %constant_dynamic-update-slice_fusion.2), channel_id=1, source_target_pairs={{0,1},{1,0},{2,3},{3,2},{4,5},{5,4},{6,7},{7,6},{8,9},{9,8},{10,11... | collective-permute-start | bytes 4718600 | tf_op jit(solution)/shard_map/ppermute | solution.py:168
  236.8 17.0 %collective-permute-start.15 = (bf16[8,256,768]{2,1,0:T(8,128)(2,1)S(1)}, bf16[8,256,768]{2,1,0:T(8,128)(2,1)S(1)}, u32[]{:S(2)}, u32[]{:S(2)}) collective-permute-start(bf16[8,256,768]{2,1,0:T(8,128)(2,1)S(1)} %constant_dynamic-update-slice_fusion.6), channel_id=1, source_target_pairs={{0,1},{1,0},{2,3},{3,2},{4,5},{5,4},{6,7},{7,6},{8,9},{9,8},{10,11... | collective-permute-start | bytes 9437192 | tf_op jit(solution)/shard_map/ppermute | solution.py:168
  244.0 20.9 %collective-permute-start.3 = (bf16[8,256,768]{2,1,0:T(8,128)(2,1)}, bf16[8,256,768]{2,1,0:T(8,128)(2,1)}, u32[]{:S(2)}, u32[]{:S(2)}) collective-permute-start(bf16[8,256,768]{2,1,0:T(8,128)(2,1)} %constant_dynamic-update-slice_fusion), channel_id=1, source_target_pairs={{0,1},{1,0},{2,3},{3,2},{4,5},{5,4},{6,7},{7,6},{8,9},{9,8},{10,11... | collective-permute-start | bytes 9437192 | tf_op jit(solution)/shard_map/ppermute | solution.py:168
  260.5 33.8 %all-to-all-start.1 = ((bf16[4,8,16,1152]{3,2,1,0:T(8,128)(2,1)}), bf16[4,8,16,1152]{3,2,1,0:T(8,128)(2,1)}, u32[]{:S(2)}, u32[]{:S(2)}) async-start(bf16[4,8,16,1152]{3,2,1,0:T(8,128)(2,1)} %bitcast.166), calls=%async_computation.1 | async-start | bytes 2359296 | tf_op jit(solution)/shard_map/all_to_all | solution.py:277
  294.4 32.2 %all-to-all-start = ((bf16[4,8,16,1152]{3,2,1,0:T(8,128)(2,1)}), bf16[4,8,16,1152]{3,2,1,0:T(8,128)(2,1)S(1)}, u32[]{:S(2)}, u32[]{:S(2)}) async-start(bf16[4,8,16,1152]{3,2,1,0:T(8,128)(2,1)} %bitcast.139), calls=%async_computation | async-start | bytes 2359296 | tf_op jit(solution)/shard_map/all_to_all | solution.py:277
  333.4 57.9 %all-to-all-start.2 = ((bf16[4,16,16,1152]{3,2,1,0:T(8,128)(2,1)}), bf16[4,16,16,1152]{3,2,1,0:T(8,128)(2,1)}, u32[]{:S(2)}, u32[]{:S(2)}) async-start(bf16[4,16,16,1152]{3,2,1,0:T(8,128)(2,1)} %bitcast.158), calls=%async_computation.2 | async-start | bytes 4718592 | tf_op jit(solution)/shard_map/all_to_all | solution.py:290
  337.9 141.9 %all-gather.5.cloned.1.call-start = ((), (), s32[]{:S(2)}) async-start(), calls=%async_computation.4 | async-start | bytes 11796480 | tf_op jit(solution)/shard_map/all_gather | solution.py:350
  394.7 68.9 %all-to-all-start.3 = ((bf16[4,128,2048]{2,1,0:T(8,128)(2,1)}), bf16[4,128,2048]{2,1,0:T(8,128)(2,1)}, u32[]{:S(2)}, u32[]{:S(2)}) async-start(bf16[4,128,2048]{2,1,0:T(8,128)(2,1)} %pad_maximum_fusion.1), calls=%async_computation.3 | async-start | bytes 4194304 | tf_op jit(solution)/shard_map/all_to_all | solution.py:339
  406.3 25.5 %collective-permute-start.18 = (bf16[4,128,2,256]{3,1,2,0:T(8,128)(2,1)S(1)}, bf16[4,128,2,256]{3,1,2,0:T(8,128)(2,1)S(1)}, u32[]{:S(2)}, u32[]{:S(2)}) collective-permute-start(bf16[4,128,2,256]{3,1,2,0:T(8,128)(2,1)S(1)} %bitcast.188), channel_id=1, source_target_pairs={{0,3},{1,2},{2,1},{3,0},{4,7},{5,6},{6,5},{7,4},{8,11},{9,10},{10,... | collective-permute-start | bytes 1572872 | tf_op jit(solution)/shard_map/ppermute | solution.py:261
  406.5 46.7 %collective-permute-start.17 = (bf16[4,128,2,256]{3,1,2,0:T(8,128)(2,1)S(1)}, bf16[4,128,2,256]{3,1,2,0:T(8,128)(2,1)S(1)}, u32[]{:S(2)}, u32[]{:S(2)}) collective-permute-start(bf16[4,128,2,256]{3,1,2,0:T(8,128)(2,1)S(1)} %bitcast.189), channel_id=1, source_target_pairs={{0,2},{1,3},{2,0},{3,1},{4,6},{5,7},{6,4},{7,5},{8,10},{9,11},{10,... | collective-permute-start | bytes 1572872 | tf_op jit(solution)/shard_map/ppermute | solution.py:261
  407.3 45.9 %collective-permute-start.16 = (bf16[4,128,2,256]{3,1,2,0:T(8,128)(2,1)S(1)}, bf16[4,128,2,256]{3,1,2,0:T(8,128)(2,1)S(1)}, u32[]{:S(2)}, u32[]{:S(2)}) collective-permute-start(bf16[4,128,2,256]{3,1,2,0:T(8,128)(2,1)S(1)} %bitcast.190), channel_id=1, source_target_pairs={{0,1},{1,0},{2,3},{3,2},{4,5},{5,4},{6,7},{7,6},{8,9},{9,8},{10,11... | collective-permute-start | bytes 1572872 | tf_op jit(solution)/shard_map/ppermute | solution.py:261
  (36 other events, 143.0 us)
Sparse Core Ops, SparseCore 0:
  55.0 46.0 all-gather.6
  394.8 84.9 all-gather.4

commit v5 on v4

--- a/solution.py
+++ b/solution.py
@@ -153,20 +153,23 @@
     return rows.reshape(shape)
 
 
-def spread_weights(weight, part, half):
+def spread_weights(weight, part, half, previous):
     group = lax.axis_index("groups")
     across = [(i, i ^ 1) for i in range(lax.axis_size("dp"))]
     beside = [(i, i ^ 2) for i in range(lax.axis_size("dp"))]
     weight = weight[2 * half * part : 2 * half * (part + 1)]
     pair = weight.reshape(2, half, *weight.shape[1:])
     own = jnp.where(group == 1, pair[::-1], pair)
-    first = lax.ppermute(own[0], "dp", beside)
+    near = own[0]
+    if previous is not None:
+        near, previous = lax.optimization_barrier((near, previous))
+    first = lax.ppermute(near, "dp", beside)
     own = own.reshape(weight.shape)
     core = lax.ppermute(own, "dp", across)
     second = lax.ppermute(first, "groups", [(0, 1), (1, 0)])
     chip = jnp.concatenate([first, second], axis=0)
     far = lax.ppermute(chip, "dp", across)
-    return own, core, chip, far
+    return (own, core, chip, far), first
 
 
 def piece_columns(rows, index, share):
@@ -202,10 +205,12 @@
     gates_group = routing[..., top_count:]
     ids_all = lax.dynamic_index_in_dim(ids_group, dp_index, 0, keepdims=False)
     gates_all = lax.dynamic_index_in_dim(gates_group, dp_index, 0, keepdims=False)
-    pieces = [
-        (spread_weights(w_gate_up, part, half), spread_weights(w_down, part, half))
-        for part in range(PARTS)
-    ]
+    pieces = []
+    previous = None
+    for part in range(PARTS):
+        gu_pieces, previous = spread_weights(w_gate_up, part, half, previous)
+        dn_pieces, previous = spread_weights(w_down, part, half, previous)
+        pieces.append((gu_pieces, dn_pieces))
 
     select, cell_gate = cell_select(ids_all, gates_all, here)
     cell_rows = pick_rows("shmt,std->hsmd", select, rows_all)
@@ -251,9 +256,7 @@
                 [d_gate.astype(jnp.bfloat16), d_up.astype(jnp.bfloat16), activation], axis=-1
             )
         )
-    last = payloads[-1]
-    rows_all, last = lax.optimization_barrier((rows_all, last))
-    payloads[-1] = last
+    rows_all, previous = lax.optimization_barrier((rows_all, previous))
     wide = rows_all.reshape(expert_peers, token_count, 2, dp_peers, share)
     narrow = [wide[..., 0, :]]
     for index in range(1, dp_peers):

time: 504 us -> 442 us (0.88)
  waiting for transfers between devices: 243 us -> 186 us
  local copies, waits for them, and re-layouts: 77.4 us -> 62.3 us
  matrix products: 81.6 us -> 88.1 us
  other arithmetic: 27.4 us -> 33.3 us
    ppermute x4, waiting for transfers between devices: 73.1 us -> 29.9 us  [spread_weights(): first = lax.ppermute(near, 'dp', beside)]
    ppermute x4, waiting for transfers between devices: 60.3 us -> 49.4 us  [spread_weights(): second = lax.ppermute(first, 'groups', [(0, 1), (1, 0)])]
    unnamed x94 -> x110, local copies, waits for them, and re-layouts: 19.9 us -> 11.8 us
    select_n x4, other arithmetic: 5.95 us -> 12.8 us  [spread_weights(): own = jnp.where(group == 1, pair[::-1], pair)]
    dot_general x8, matrix products: 12.9 us -> 18.8 us  [shared_shards(): jnp.einsum('hrd,hdf->hrf', piece_columns(arrived[span], index, share), gu...]
  transfers between devices with their start and end apart: 25 -> 25, of which waited for: 11 -> 14; matrix products, arithmetic and copies ran while one was open for 28% -> 34% of each run, Pallas kernels for 0% -> 0%
where the time goes in v5:
time: 442 us; the launch traced here: 437 us
  waiting for transfers between devices  186 us (42%)
  matrix products  88.1 us (20%)
  local copies, waits for them, and re-layouts  62.3 us (14%)
  other arithmetic  33.3 us (8%)
  starting transfers between devices  29.3 us (7%)
  blocking collectives  23.4 us (5%)
  between operations  15.2 us (3%)
    ppermute x4, waiting for transfers between devices, spread_weights(): second = lax.ppermute(first, 'groups', [(0, 1), (1, 0)])  49.4 us
    ppermute x3, waiting for transfers between devices, shared_shards(): narrow.append(lax.ppermute(wide[..., index, :], 'dp', partners))  43.9 us
    ppermute x4, waiting for transfers between devices, spread_weights(): first = lax.ppermute(near, 'dp', beside)  29.9 us
    all_to_all x1, waiting for transfers between devices, shared_shards(): lax.all_to_all(spread, 'expert', split_axis=0, concat_axis=0, tiled=True)  29.3 us
    all_to_all x2, waiting for transfers between devices, shared_shards(): lax.all_to_all(jnp.transpose(part_payload.reshape(pay_shape), (1, 0, 2, 3...  25.3 us
    all_gather x1, blocking collectives, shared_shards(): routing = lax.all_gather(routing, ('expert', 'dp'), axis=0, tiled=False)  23.4 us
    dot_general x8, matrix products, shared_shards(): jnp.einsum('hrf,hdf->hrd', part_payload[..., :2 * hidden_width], piece, p...  22.9 us
    dot_general x8, matrix products, shared_shards(): jnp.einsum('hrd,hdf->hrf', piece_columns(arrived[span], index, share), gu...  18.8 us
  transfers between devices with their start and end apart: 25, of which 14 were waited for; matrix products, arithmetic and copies ran while one was open for 34% of the time, Pallas kernels for 0%

profile of v5, /device:TPU:0, one launch (start us, length us, event | category | flops | bytes accessed | tf_op | source)
XLA Modules:
  0.0 437.1 jit_solution(295775595032696153)
XLA Ops:
  8.6 23.4 %all-gather = f32[256,128]{1,0:T(8,128)S(1)} all-gather(f32[16,128]{1,0:T(8,128)S(1)} %pad_maximum_fusion.8), channel_id=2, replica_groups=mesh['groups'=2,'expert'=4,'dp'=4] {'expert','dp'}, dimensions={0}, use_global_device_ids=true | all-gather | bytes 139264 | tf_op jit(solution)/shard_map/all_gather | solution.py:199
  32.0 6.1 %fusion.60 = (bf16[8,256,768]{2,1,0:T(8,128)(2,1)}, bf16[8,256,768]{2,1,0:T(8,128)(2,1)}) fusion(bf16[16,256,768]{2,1,0:T(8,128)(2,1)} %param.10), kind=kLoop, calls=%fused_computation.153 | loop fusion | bytes 12582912 | tf_op jit(solution)/shard_map/slice | solution.py:160
  38.1 3.6 reverse_select_fusion.1
  54.6 5.4 %reverse_select_fusion = bf16[2,4,256,768]{3,2,1,0:T(8,128)(2,1)} fusion(bf16[2,4,256,768]{3,2,1,0:T(8,128)(2,1)} %bitcast.155, pred[]{:T(512)S(6)} %eq.89), kind=kLoop, calls=%fused_computation.3 | loop fusion | flops 1572864 | bytes 6291457 | tf_op jit(solution)/shard_map/jit(_where)/select_n | solution.py:162
  71.6 8.4 %collective-permute-done.1 = bf16[4,256,768]{2,1,0:T(8,128)(2,1)} collective-permute-done((bf16[4,256,768]{2,1,0:T(8,128)(2,1)}, bf16[4,256,768]{2,1,0:T(8,128)(2,1)}, u32[]{:S(2)}, u32[]{:S(2)}) %collective-permute-start.1) | collective-permute-done | bytes 1572896 | tf_op jit(solution)/shard_map/ppermute | solution.py:166
  89.3 9.7 %collective-permute-done.5 = bf16[4,384,256]{2,1,0:T(8,128)(2,1)S(1)} collective-permute-done((bf16[4,384,256]{2,1,0:T(8,128)(2,1)S(1)}, bf16[4,384,256]{2,1,0:T(8,128)(2,1)S(1)}, u32[]{:S(2)}, u32[]{:S(2)}) %collective-permute-start.5) | collective-permute-done | bytes 786464 | tf_op jit(solution)/shard_map/ppermute | solution.py:166
  105.3 15.9 %collective-permute-done.2 = bf16[4,256,768]{2,1,0:T(8,128)(2,1)} collective-permute-done((bf16[4,256,768]{2,1,0:T(8,128)(2,1)}, bf16[4,256,768]{2,1,0:T(8,128)(2,1)}, u32[]{:S(2)}, u32[]{:S(2)}) %collective-permute-start.2) | collective-permute-done | bytes 1572896 | tf_op jit(solution)/shard_map/ppermute | solution.py:169
  124.3 4.9 %fusion.44 = f32[8,64,768]{2,1,0:T(8,128)} fusion(bf16[8,256,768]{2,1,0:T(8,128)(2,1)} %bitcast.25, bf16[8,64,1024]{2,1,0:T(8,128)(2,1)S(1)} %bitcast.171), kind=kOutput, calls=%fused_computation.121 | convolution fusion | flops 201326592 | bytes 4980736 | tf_op jit(solution)/shard_map/hrd,hdf->hrf/dot_general | solution.py:230
  131.3 8.1 %collective-permute-done.6 = bf16[4,384,256]{2,1,0:T(8,128)(2,1)S(1)} collective-permute-done((bf16[4,384,256]{2,1,0:T(8,128)(2,1)S(1)}, bf16[4,384,256]{2,1,0:T(8,128)(2,1)S(1)}, u32[]{:S(2)}, u32[]{:S(2)}) %collective-permute-start.6) | collective-permute-done | bytes 786464 | tf_op jit(solution)/shard_map/ppermute | solution.py:169
  146.8 3.8 fusion.42
  153.1 11.7 %collective-permute-done.13 = bf16[4,384,256]{2,1,0:T(8,128)(2,1)S(1)} collective-permute-done((bf16[4,384,256]{2,1,0:T(8,128)(2,1)S(1)}, bf16[4,384,256]{2,1,0:T(8,128)(2,1)S(1)}, u32[]{:S(2)}, u32[]{:S(2)}) %collective-permute-start.13) | collective-permute-done | bytes 786464 | tf_op jit(solution)/shard_map/ppermute | solution.py:166
  168.9 11.8 %collective-permute-done.10 = bf16[4,256,768]{2,1,0:T(8,128)(2,1)S(1)} collective-permute-done((bf16[4,256,768]{2,1,0:T(8,128)(2,1)}, bf16[4,256,768]{2,1,0:T(8,128)(2,1)S(1)}, u32[]{:S(2)}, u32[]{:S(2)}) %collective-permute-start.10) | collective-permute-done | bytes 1572896 | tf_op jit(solution)/shard_map/ppermute | solution.py:169
  183.5 13.6 %collective-permute-done.14 = bf16[4,384,256]{2,1,0:T(8,128)(2,1)S(1)} collective-permute-done((bf16[4,384,256]{2,1,0:T(8,128)(2,1)S(1)}, bf16[4,384,256]{2,1,0:T(8,128)(2,1)S(1)}, u32[]{:S(2)}, u32[]{:S(2)}) %collective-permute-start.14) | collective-permute-done | bytes 786464 | tf_op jit(solution)/shard_map/ppermute | solution.py:169
  202.7 4.3 all-to-all-start
  223.7 12.8 %all-to-all-done = bf16[4,8,16,1152]{3,2,1,0:T(8,128)(2,1)} async-done(((bf16[4,8,16,1152]{3,2,1,0:T(8,128)(2,1)}), bf16[4,8,16,1152]{3,2,1,0:T(8,128)(2,1)}, u32[]{:S(2)}, u32[]{:S(2)}) %all-to-all-start) | async-done | bytes 1179680 | tf_op jit(solution)/shard_map/all_to_all | solution.py:280
  236.5 4.3 all-to-all-start.1
  243.6 3.7 convolution_convert_fusion.5
  250.9 3.7 convolution_convert_fusion.6
  257.1 12.5 %all-to-all-done.1 = bf16[4,8,16,1152]{3,2,1,0:T(8,128)(2,1)} async-done(((bf16[4,8,16,1152]{3,2,1,0:T(8,128)(2,1)}), bf16[4,8,16,1152]{3,2,1,0:T(8,128)(2,1)}, u32[]{:S(2)}, u32[]{:S(2)}) %all-to-all-start.1) | async-done | bytes 1179680 | tf_op jit(solution)/shard_map/all_to_all | solution.py:280
  273.7 3.6 all-to-all-start.2
  282.9 3.0 convolution_convert_fusion.1
  285.8 3.0 convolution_convert_fusion.3
  291.8 3.0 convolution_convert_fusion.2
  301.4 29.3 %all-to-all-done.2 = bf16[4,16,16,1152]{3,2,1,0:T(8,128)(2,1)S(1)} async-done(((bf16[4,16,16,1152]{3,2,1,0:T(8,128)(2,1)}), bf16[4,16,16,1152]{3,2,1,0:T(8,128)(2,1)S(1)}, u32[]{:S(2)}, u32[]{:S(2)}) %all-to-all-start.2) | async-done | bytes 2359328 | tf_op jit(solution)/shard_map/all_to_all | solution.py:293
  332.4 4.6 %all-to-all-start.3 = ((bf16[4,128,2048]{2,1,0:T(8,128)(2,1)}), bf16[4,128,2048]{2,1,0:T(8,128)(2,1)}, u32[]{:S(2)}, u32[]{:S(2)}) async-start(bf16[4,128,2048]{2,1,0:T(8,128)(2,1)} %pad_maximum_fusion.1), calls=%async_computation.3 | async-start | bytes 4194304 | tf_op jit(solution)/shard_map/all_to_all | solution.py:342
  337.3 3.5 reshape.170
  340.7 3.2 fusion.63
  347.5 22.0 %collective-permute-done.18 = bf16[4,128,2,256]{3,1,2,0:T(8,128)(2,1)S(1)} collective-permute-done((bf16[4,128,2,256]{3,1,2,0:T(8,128)(2,1)S(1)}, bf16[4,128,2,256]{3,1,2,0:T(8,128)(2,1)S(1)}, u32[]{:S(2)}, u32[]{:S(2)}) %collective-permute-start.18) | collective-permute-done | bytes 524320 | tf_op jit(solution)/shard_map/ppermute | solution.py:264
  369.5 22.0 %collective-permute-done.17 = bf16[4,128,2,256]{3,1,2,0:T(8,128)(2,1)S(1)} collective-permute-done((bf16[4,128,2,256]{3,1,2,0:T(8,128)(2,1)S(1)}, bf16[4,128,2,256]{3,1,2,0:T(8,128)(2,1)S(1)}, u32[]{:S(2)}, u32[]{:S(2)}) %collective-permute-start.17) | collective-permute-done | bytes 524320 | tf_op jit(solution)/shard_map/ppermute | solution.py:264
  410.8 7.1 %all-gather.5.cloned.1.call-done = bf16[16,256,1152]{2,1,0:T(8,128)(2,1)} async-done(((bf16[16,64,1152]{2,1,0:T(8,128)(2,1)}), bf16[16,256,1152]{2,1,0:T(8,128)(2,1)}) %all-gather.5.cloned.1.call-update) | async-done | bytes 9437200 | tf_op jit(solution)/shard_map/all_gather | solution.py:353
  417.9 7.5 %fusion.5 = bf16[16,256,768]{2,1,0:T(8,128)(2,1)} fusion(bf16[16,256,256]{2,1,0:T(8,128)(2,1)S(1)} %bitcast.161, bf16[16,256,1152]{2,1,0:T(8,128)(2,1)} %all-gather.5.cloned.1.call-done), kind=kOutput, calls=%fused_computation.13 | convolution fusion | flops 1613758464 | bytes 14680064 | tf_op jit(solution)/shard_map/hrc,hrf->hcf/dot_general | solution.py:354
  425.4 4.7 %fusion.10 = bf16[16,384,256]{2,1,0:T(8,128)(2,1)} fusion(bf16[16,256,256]{2,1,0:T(8,128)(2,1)S(1)} %bitcast.164, bf16[16,256,1152]{2,1,0:T(8,128)(2,1)} %all-gather.5.cloned.1.call-done), kind=kOutput, calls=%fused_computation.22 | convolution fusion | flops 806879232 | bytes 8388608 | tf_op jit(solution)/shard_map/hrf,hrc->hfc/dot_general | solution.py:360
  (254 shorter events, 137.9 us)
Async XLA Ops:
  7.2 94.3 %all-gather.7.cloned.1.call-start = ((), (), s32[]{:S(2)}) async-start(), calls=%async_computation.5 | async-start | bytes 2621440 | tf_op jit(solution)/shard_map/all_gather | solution.py:197
  43.0 37.0 %collective-permute-start.1 = (bf16[4,256,768]{2,1,0:T(8,128)(2,1)}, bf16[4,256,768]{2,1,0:T(8,128)(2,1)}, u32[]{:S(2)}, u32[]{:S(2)}) collective-permute-start(bf16[4,256,768]{2,1,0:T(8,128)(2,1)} %slice_bitcast_fusion.1), channel_id=1, source_target_pairs={{0,2},{1,3},{2,0},{3,1},{4,6},{5,7},{6,4},{7,5},{8,10},{9,11},{10,... | collective-permute-start | bytes 4718600 | tf_op jit(solution)/shard_map/ppermute | solution.py:166
  60.0 84.8 %collective-permute-start.8 = (bf16[8,256,768]{2,1,0:T(8,128)(2,1)}, bf16[8,256,768]{2,1,0:T(8,128)(2,1)}, u32[]{:S(2)}, u32[]{:S(2)}) collective-permute-start(bf16[8,256,768]{2,1,0:T(8,128)(2,1)} %bitcast.25), channel_id=1, source_target_pairs={{0,1},{1,0},{2,3},{3,2},{4,5},{5,4},{6,7},{7,6},{8,9},{9,8},{10,11... | collective-permute-start | bytes 9437192 | tf_op jit(solution)/shard_map/ppermute | solution.py:168
  65.1 64.0 %collective-permute-start.12 = (bf16[8,384,256]{2,1,0:T(8,128)(2,1)}, bf16[8,384,256]{2,1,0:T(8,128)(2,1)}, u32[]{:S(2)}, u32[]{:S(2)}) collective-permute-start(bf16[8,384,256]{2,1,0:T(8,128)(2,1)} %bitcast.28), channel_id=1, source_target_pairs={{0,1},{1,0},{2,3},{3,2},{4,5},{5,4},{6,7},{7,6},{8,9},{9,8},{10,11... | collective-permute-start | bytes 4718600 | tf_op jit(solution)/shard_map/ppermute | solution.py:168
  65.2 80.0 %collective-permute-start = (bf16[8,256,768]{2,1,0:T(8,128)(2,1)S(1)}, bf16[8,256,768]{2,1,0:T(8,128)(2,1)}, u32[]{:S(2)}, u32[]{:S(2)}) collective-permute-start(bf16[8,256,768]{2,1,0:T(8,128)(2,1)S(1)} %bitcast.148), channel_id=1, source_target_pairs={{0,1},{1,0},{2,3},{3,2},{4,5},{5,4},{6,7},{7,6},{8,9},{9,8},{10,11... | collective-permute-start | bytes 9437192 | tf_op jit(solution)/shard_map/ppermute | solution.py:168
  68.9 32.5 %copy-start.46 = (s32[4,16,128]{2,1,0:T(8,128)}, s32[4,16,128]{2,1,0:T(8,128)S(1)}, u32[]{:S(2)}) copy-start(s32[4,16,128]{2,1,0:T(8,128)S(1)} %fusion.21) | copy-start | bytes 98308
  69.2 35.4 %copy-start.48 = (f32[4,16,16]{2,1,0:T(8,128)}, f32[4,16,16]{2,1,0:T(8,128)S(1)}, u32[]{:S(2)}) copy-start(f32[4,16,16]{2,1,0:T(8,128)S(1)} %select_reduce_fusion.1) | copy-start | bytes 12292
  80.0 19.0 %collective-permute-start.5 = (bf16[4,384,256]{2,1,0:T(8,128)(2,1)S(1)}, bf16[4,384,256]{2,1,0:T(8,128)(2,1)S(1)}, u32[]{:S(2)}, u32[]{:S(2)}) collective-permute-start(bf16[4,384,256]{2,1,0:T(8,128)(2,1)S(1)} %slice_bitcast_fusion.3), channel_id=1, source_target_pairs={{0,2},{1,3},{2,0},{3,1},{4,6},{5,7},{6,4},{7,5},{8,10},{9,11},{10,... | collective-permute-start | bytes 2359304 | tf_op jit(solution)/shard_map/ppermute | solution.py:166
  85.1 36.2 %collective-permute-start.2 = (bf16[4,256,768]{2,1,0:T(8,128)(2,1)}, bf16[4,256,768]{2,1,0:T(8,128)(2,1)}, u32[]{:S(2)}, u32[]{:S(2)}) collective-permute-start(bf16[4,256,768]{2,1,0:T(8,128)(2,1)} %collective-permute-done.1), channel_id=1, source_target_pairs={{0,16},{16,0},{1,17},{17,1},{2,18},{18,2},{3,19},{19,3},{4,20},{20... | collective-permute-start | bytes 4718600 | tf_op jit(solution)/shard_map/ppermute | solution.py:169
  99.0 44.2 %collective-permute-start.9 = (bf16[4,256,768]{2,1,0:T(8,128)(2,1)}, bf16[4,256,768]{2,1,0:T(8,128)(2,1)}, u32[]{:S(2)}, u32[]{:S(2)}) collective-permute-start(bf16[4,256,768]{2,1,0:T(8,128)(2,1)} %slice_bitcast_fusion), channel_id=1, source_target_pairs={{0,2},{1,3},{2,0},{3,1},{4,6},{5,7},{6,4},{7,5},{8,10},{9,11},{10,... | collective-permute-start | bytes 4718600 | tf_op jit(solution)/shard_map/ppermute | solution.py:166
  105.1 17.7 %copy-start = (bf16[8,256,768]{2,1,0:T(8,128)(2,1)S(1)}, bf16[8,256,768]{2,1,0:T(8,128)(2,1)}, u32[]{:S(2)}) copy-start(bf16[8,256,768]{2,1,0:T(8,128)(2,1)} %constant_dynamic-update-slice_fusion.1) | copy-start | bytes 9437188
  105.2 41.6 %copy-start.22 = (bf16[8,4,16,1024]{3,2,1,0:T(8,128)(2,1)}, bf16[8,4,16,1024]{3,2,1,0:T(8,128)(2,1)S(1)}, u32[]{:S(2)}) copy-start(bf16[8,4,16,1024]{3,2,1,0:T(8,128)(2,1)S(1)} %copy.63) | copy-start | bytes 3145732
  105.3 34.1 %copy-start.26 = (bf16[8,4,16,1024]{3,2,1,0:T(8,128)(2,1)}, bf16[8,4,16,1024]{3,2,1,0:T(8,128)(2,1)S(1)}, u32[]{:S(2)}) copy-start(bf16[8,4,16,1024]{3,2,1,0:T(8,128)(2,1)S(1)} %copy.66) | copy-start | bytes 3145732
  121.3 18.1 %collective-permute-start.6 = (bf16[4,384,256]{2,1,0:T(8,128)(2,1)S(1)}, bf16[4,384,256]{2,1,0:T(8,128)(2,1)S(1)}, u32[]{:S(2)}, u32[]{:S(2)}) collective-permute-start(bf16[4,384,256]{2,1,0:T(8,128)(2,1)S(1)} %copy-done.40), channel_id=1, source_target_pairs={{0,16},{16,0},{1,17},{17,1},{2,18},{18,2},{3,19},{19,3},{4,20},{20... | collective-permute-start | bytes 2359304 | tf_op jit(solution)/shard_map/ppermute | solution.py:169
  124.3 74.5 %copy-start.1 = (bf16[8,256,768]{2,1,0:T(8,128)(2,1)}, bf16[8,256,768]{2,1,0:T(8,128)(2,1)S(1)}, u32[]{:S(2)}) copy-start(bf16[8,256,768]{2,1,0:T(8,128)(2,1)S(1)} %constant_dynamic-update-slice_fusion) | copy-start | bytes 9437188
  129.2 68.9 %collective-permute-start.3 = (bf16[8,256,768]{2,1,0:T(8,128)(2,1)S(1)}, bf16[8,256,768]{2,1,0:T(8,128)(2,1)S(1)}, u32[]{:S(2)}, u32[]{:S(2)}) collective-permute-start(bf16[8,256,768]{2,1,0:T(8,128)(2,1)S(1)} %constant_dynamic-update-slice_fusion), channel_id=1, source_target_pairs={{0,1},{1,0},{2,3},{3,2},{4,5},{5,4},{6,7},{7,6},{8,9},{9,8},{10,11... | collective-permute-start | bytes 9437192 | tf_op jit(solution)/shard_map/ppermute | solution.py:171
  139.4 26.2 %collective-permute-start.4 = (bf16[8,384,256]{2,1,0:T(8,128)(2,1)S(1)}, bf16[8,384,256]{2,1,0:T(8,128)(2,1)S(1)}, u32[]{:S(2)}, u32[]{:S(2)}) collective-permute-start(bf16[8,384,256]{2,1,0:T(8,128)(2,1)S(1)} %bitcast.151), channel_id=1, source_target_pairs={{0,1},{1,0},{2,3},{3,2},{4,5},{5,4},{6,7},{7,6},{8,9},{9,8},{10,11... | collective-permute-start | bytes 4718600 | tf_op jit(solution)/shard_map/ppermute | solution.py:168
  143.2 37.5 %collective-permute-start.10 = (bf16[4,256,768]{2,1,0:T(8,128)(2,1)}, bf16[4,256,768]{2,1,0:T(8,128)(2,1)S(1)}, u32[]{:S(2)}, u32[]{:S(2)}) collective-permute-start(bf16[4,256,768]{2,1,0:T(8,128)(2,1)} %collective-permute-done.9), channel_id=1, source_target_pairs={{0,16},{16,0},{1,17},{17,1},{2,18},{18,2},{3,19},{19,3},{4,20},{20... | collective-permute-start | bytes 4718600 | tf_op jit(solution)/shard_map/ppermute | solution.py:169
  144.8 55.8 %copy-start.25 = (bf16[8,384,256]{2,1,0:T(8,128)(2,1)}, bf16[8,384,256]{2,1,0:T(8,128)(2,1)S(1)}, u32[]{:S(2)}) copy-start(bf16[8,384,256]{2,1,0:T(8,128)(2,1)S(1)} %constant_dynamic-update-slice_fusion.2) | copy-start | bytes 4718596
  144.8 38.0 %collective-permute-start.7 = (bf16[8,384,256]{2,1,0:T(8,128)(2,1)S(1)}, bf16[8,384,256]{2,1,0:T(8,128)(2,1)S(1)}, u32[]{:S(2)}, u32[]{:S(2)}) collective-permute-start(bf16[8,384,256]{2,1,0:T(8,128)(2,1)S(1)} %constant_dynamic-update-slice_fusion.2), channel_id=1, source_target_pairs={{0,1},{1,0},{2,3},{3,2},{4,5},{5,4},{6,7},{7,6},{8,9},{9,8},{10,11... | collective-permute-start | bytes 4718600 | tf_op jit(solution)/shard_map/ppermute | solution.py:171
  145.1 19.7 %collective-permute-start.13 = (bf16[4,384,256]{2,1,0:T(8,128)(2,1)S(1)}, bf16[4,384,256]{2,1,0:T(8,128)(2,1)S(1)}, u32[]{:S(2)}, u32[]{:S(2)}) collective-permute-start(bf16[4,384,256]{2,1,0:T(8,128)(2,1)S(1)} %copy-done.38), channel_id=1, source_target_pairs={{0,2},{1,3},{2,0},{3,1},{4,6},{5,7},{6,4},{7,5},{8,10},{9,11},{10,... | collective-permute-start | bytes 2359304 | tf_op jit(solution)/shard_map/ppermute | solution.py:166
  164.9 32.3 %collective-permute-start.14 = (bf16[4,384,256]{2,1,0:T(8,128)(2,1)S(1)}, bf16[4,384,256]{2,1,0:T(8,128)(2,1)S(1)}, u32[]{:S(2)}, u32[]{:S(2)}) collective-permute-start(bf16[4,384,256]{2,1,0:T(8,128)(2,1)S(1)} %collective-permute-done.13), channel_id=1, source_target_pairs={{0,16},{16,0},{1,17},{17,1},{2,18},{18,2},{3,19},{19,3},{4,20},{20... | collective-permute-start | bytes 2359304 | tf_op jit(solution)/shard_map/ppermute | solution.py:169
  181.9 32.0 %collective-permute-start.11 = (bf16[8,256,768]{2,1,0:T(8,128)(2,1)}, bf16[8,256,768]{2,1,0:T(8,128)(2,1)}, u32[]{:S(2)}, u32[]{:S(2)}) collective-permute-start(bf16[8,256,768]{2,1,0:T(8,128)(2,1)} %constant_dynamic-update-slice_fusion.4), channel_id=1, source_target_pairs={{0,1},{1,0},{2,3},{3,2},{4,5},{5,4},{6,7},{7,6},{8,9},{9,8},{10,11... | collective-permute-start | bytes 9437192 | tf_op jit(solution)/shard_map/ppermute | solution.py:171
  198.1 13.9 %collective-permute-start.15 = (bf16[8,384,256]{2,1,0:T(8,128)(2,1)}, bf16[8,384,256]{2,1,0:T(8,128)(2,1)}, u32[]{:S(2)}, u32[]{:S(2)}) collective-permute-start(bf16[8,384,256]{2,1,0:T(8,128)(2,1)} %constant_dynamic-update-slice_fusion.6), channel_id=1, source_target_pairs={{0,1},{1,0},{2,3},{3,2},{4,5},{5,4},{6,7},{7,6},{8,9},{9,8},{10,11... | collective-permute-start | bytes 4718600 | tf_op jit(solution)/shard_map/ppermute | solution.py:171
  202.7 33.8 %all-to-all-start = ((bf16[4,8,16,1152]{3,2,1,0:T(8,128)(2,1)}), bf16[4,8,16,1152]{3,2,1,0:T(8,128)(2,1)}, u32[]{:S(2)}, u32[]{:S(2)}) async-start(bf16[4,8,16,1152]{3,2,1,0:T(8,128)(2,1)} %bitcast.167), calls=%async_computation | async-start | bytes 2359296 | tf_op jit(solution)/shard_map/all_to_all | solution.py:280
  236.5 33.1 %all-to-all-start.1 = ((bf16[4,8,16,1152]{3,2,1,0:T(8,128)(2,1)}), bf16[4,8,16,1152]{3,2,1,0:T(8,128)(2,1)}, u32[]{:S(2)}, u32[]{:S(2)}) async-start(bf16[4,8,16,1152]{3,2,1,0:T(8,128)(2,1)} %bitcast.168), calls=%async_computation.1 | async-start | bytes 2359296 | tf_op jit(solution)/shard_map/all_to_all | solution.py:280
  273.7 56.9 %all-to-all-start.2 = ((bf16[4,16,16,1152]{3,2,1,0:T(8,128)(2,1)}), bf16[4,16,16,1152]{3,2,1,0:T(8,128)(2,1)S(1)}, u32[]{:S(2)}, u32[]{:S(2)}) async-start(bf16[4,16,16,1152]{3,2,1,0:T(8,128)(2,1)} %bitcast.159), calls=%async_computation.2 | async-start | bytes 4718592 | tf_op jit(solution)/shard_map/all_to_all | solution.py:293
  277.3 140.6 %all-gather.5.cloned.1.call-start = ((), (), s32[]{:S(2)}) async-start(), calls=%async_computation.4 | async-start | bytes 11796480 | tf_op jit(solution)/shard_map/all_gather | solution.py:353
  332.4 69.3 %all-to-all-start.3 = ((bf16[4,128,2048]{2,1,0:T(8,128)(2,1)}), bf16[4,128,2048]{2,1,0:T(8,128)(2,1)}, u32[]{:S(2)}, u32[]{:S(2)}) async-start(bf16[4,128,2048]{2,1,0:T(8,128)(2,1)} %pad_maximum_fusion.1), calls=%async_computation.3 | async-start | bytes 4194304 | tf_op jit(solution)/shard_map/all_to_all | solution.py:342
  344.0 25.5 %collective-permute-start.18 = (bf16[4,128,2,256]{3,1,2,0:T(8,128)(2,1)S(1)}, bf16[4,128,2,256]{3,1,2,0:T(8,128)(2,1)S(1)}, u32[]{:S(2)}, u32[]{:S(2)}) collective-permute-start(bf16[4,128,2,256]{3,1,2,0:T(8,128)(2,1)S(1)} %bitcast.191), channel_id=1, source_target_pairs={{0,3},{1,2},{2,1},{3,0},{4,7},{5,6},{6,5},{7,4},{8,11},{9,10},{10,... | collective-permute-start | bytes 1572872 | tf_op jit(solution)/shard_map/ppermute | solution.py:264
  344.2 47.3 %collective-permute-start.17 = (bf16[4,128,2,256]{3,1,2,0:T(8,128)(2,1)S(1)}, bf16[4,128,2,256]{3,1,2,0:T(8,128)(2,1)S(1)}, u32[]{:S(2)}, u32[]{:S(2)}) collective-permute-start(bf16[4,128,2,256]{3,1,2,0:T(8,128)(2,1)S(1)} %bitcast.192), channel_id=1, source_target_pairs={{0,2},{1,3},{2,0},{3,1},{4,6},{5,7},{6,4},{7,5},{8,10},{9,11},{10,... | collective-permute-start | bytes 1572872 | tf_op jit(solution)/shard_map/ppermute | solution.py:264
  345.4 46.1 %collective-permute-start.16 = (bf16[4,128,2,256]{3,1,2,0:T(8,128)(2,1)S(1)}, bf16[4,128,2,256]{3,1,2,0:T(8,128)(2,1)S(1)}, u32[]{:S(2)}, u32[]{:S(2)}) collective-permute-start(bf16[4,128,2,256]{3,1,2,0:T(8,128)(2,1)S(1)} %bitcast.193), channel_id=1, source_target_pairs={{0,1},{1,0},{2,3},{3,2},{4,5},{5,4},{6,7},{7,6},{8,9},{9,8},{10,11... | collective-permute-start | bytes 1572872 | tf_op jit(solution)/shard_map/ppermute | solution.py:264
  (44 other events, 161.6 us)
Sparse Core Ops, SparseCore 0:
  54.7 46.6 all-gather.6
  332.5 85.3 all-gather.4
